TPU v7x, 1024 devices: a whole 4x8x16 slice. The times are simulated.
1024 devices in a mesh: row: 32 (over z_lo, y), col: 32 (over x, z_hi, core).
Axes of the slice: x: 4, y: 8, z: 16 (z_hi: 4, z_lo: 4; z = z_hi * 4 + z_lo), core: 2. Of those that a mesh axis runs over, the one named last changes fastest.
Arguments:
- a_panels: float32 [32, 32, 3, 256, 256], P('row', 'col'), may hold values from -0.375 to 0.375
- a_index: int32 [32, 32, 3], P('row', 'col'), may hold values from 0 to 16, as said below
- b_panels: float32 [32, 32, 3, 256, 256], P('row', 'col'), may hold values from -6 to 6
- b_index: int32 [32, 32, 3], P('row', 'col'), may hold values from 0 to 16, as said below
- c_index: int32 [32, 32, 6], P('row', 'col'), may hold values from 0 to 15, as said below
Outputs:
- product_blocks: float32 [32, 32, 6, 256, 256], P('row', 'col')
Inputs may be any that keep to these rules, and one draw needn't show every extreme that they name: `a_index`: within one panel the occupied slots come first and hold distinct positions; every panel has at least one occupied slot; some panel is full and some is padded. `b_index`: within one panel the occupied slots come first and hold distinct positions; every panel has at least one occupied slot; some panel is full and some is padded. `c_index`: the 6 positions of one device are distinct.
All inputs are finite; a program needn't handle non-finite values.
Results may differ from a plain program's by a relative error of at most 0.0003.
Values sent between devices are 32-bit elements; how exact they have to be, the bound alone decides.
A program may use at most 128 MiB of HBM per device.

v0:
```python
import jax
import jax.numpy as jnp
from jax import lax
from jax.sharding import PartitionSpec as P

RB = 4
CB = 4
KB = 4


def passed_along(array, axis, by):
    peers = lax.axis_size(axis)
    return lax.ppermute(array, axis, [(i, (i + by) % peers) for i in range(peers)])


def match_table(a_slots, b_slots, c_slots):
    a_valid = a_slots < RB * KB
    a_inner = a_slots % KB
    a_row = a_slots // KB
    b_valid = b_slots < KB * CB
    b_inner = b_slots // CB
    b_col = b_slots % CB
    matched = (a_inner[:, None] == b_inner[None, :]) & a_valid[:, None] & b_valid[None, :]
    target = a_row[:, None] * CB + b_col[None, :]
    return (target[None, :, :] == c_slots[:, None, None]) & matched[None, :, :]


def pair_product(a_blocks, a_slots, b_blocks, b_slots, c_slots):
    prods = jnp.einsum("pxy,qyz->pqxz", a_blocks, b_blocks, precision=lax.Precision.HIGHEST)
    select = match_table(a_slots, b_slots, c_slots).astype(jnp.float32)
    return jnp.einsum("fpq,pqxz->fxz", select, prods, precision=lax.Precision.HIGHEST)


def per_device(a_panels, a_index, b_panels, b_index, c_index):
    a_here = a_panels[0, 0]
    a_slots = a_index[0, 0]
    b_here = b_panels[0, 0]
    b_slots = b_index[0, 0]
    c_slots = c_index[0, 0]
    a_moved, a_moved_slots = passed_along((a_here, a_slots), "col", -1)
    b_moved, b_moved_slots = passed_along((b_here, b_slots), "row", -1)
    total = pair_product(a_here, a_slots, b_here, b_slots, c_slots) + pair_product(
        a_moved, a_moved_slots, b_moved, b_moved_slots, c_slots
    )
    return total[None, None]


def solution(mesh):
    return jax.shard_map(
        per_device,
        mesh=mesh,
        in_specs=(
            P("row", "col", None, None, None),
            P("row", "col", None),
            P("row", "col", None, None, None),
            P("row", "col", None),
            P("row", "col", None),
        ),
        out_specs=P("row", "col", None, None, None),
        check_vma=False,
    )
```

profile of v0, /device:TPU:199, one launch (start us, length us, event | category | flops | bytes accessed | tf_op | source)
XLA Modules:
  0.0 86.4 jit_solution(17190028194471039952)
XLA Ops:
  0.0 0.0 copy-start.1
  0.0 0.0 copy-start.2
  0.0 4.3 %collective-permute-start.2 = (f32[3,256,256]{2,1,0:T(8,128)}, f32[3,256,256]{2,1,0:T(8,128)}, u32[]{:S(2)}, u32[]{:S(2)}) collective-permute-start(f32[3,256,256]{2,1,0:T(8,128)} %bitcast.61), channel_id=1, source_target_pairs={{0,992},{32,0},{64,32},{96,64},{128,96},{160,128},{192,160},{224,1... | collective-permute-start | bytes 2359304 | tf_op jit(solution)/shard_map/ppermute | solution.py:13
  4.3 2.9 %collective-permute-start.3 = (f32[3,256,256]{2,1,0:T(8,128)}, f32[3,256,256]{2,1,0:T(8,128)}, u32[]{:S(2)}, u32[]{:S(2)}) collective-permute-start(f32[3,256,256]{2,1,0:T(8,128)} %bitcast.62), channel_id=1, source_target_pairs={{0,31},{1,0},{2,1},{3,2},{4,3},{5,4},{6,5},{7,6},{8,7},{9,8},{10,9... | collective-permute-start | bytes 2359304 | tf_op jit(solution)/shard_map/ppermute | solution.py:13
  7.2 3.0 %collective-permute-start.1 = (s32[3]{0:T(128)}, s32[3]{0:T(128)S(1)}, u32[]{:S(2)}, u32[]{:S(2)}) collective-permute-start(s32[3]{0:T(128)} %bitcast.65), channel_id=1, source_target_pairs={{0,992},{32,0},{64,32},{96,64},{128,96},{160,128},{192,160},{224,1... | collective-permute-start | bytes 44 | tf_op jit(solution)/shard_map/ppermute | solution.py:13
  10.2 16.1 %collective-permute-start = (s32[3]{0:T(128)}, s32[3]{0:T(128)S(1)}, u32[]{:S(2)}, u32[]{:S(2)}) collective-permute-start(s32[3]{0:T(128)} %bitcast.66), channel_id=1, source_target_pairs={{0,31},{1,0},{2,1},{3,2},{4,3},{5,4},{6,5},{7,6},{8,7},{9,8},{10,9... | collective-permute-start | bytes 44 | tf_op jit(solution)/shard_map/ppermute | solution.py:13
  26.3 6.6 %fusion.9 = f32[3,256,3,256]{3,1,2,0:T(8,128)} fusion(f32[1,1,3,256,256]{4,3,2,1,0:T(8,128)} %param.5, f32[1,1,3,256,256]{4,3,2,1,0:T(8,128)} %param.7), kind=kOutput, calls=%fused_computation.8 | convolution fusion | flops 1811939328 | bytes 3932160 | tf_op jit(solution)/shard_map/pxy,qyz->pqxz/dot_general | solution.py:29
  32.9 0.0 copy-done.1
  32.9 0.0 copy-done.2
  33.0 3.3 %copy.8 = f32[3,256,3,256]{1,0,2,3:T(4,128)S(1)} copy(f32[3,256,3,256]{3,1,2,0:T(8,128)} %fusion.9) | data formatting | bytes 4718592 | tf_op jit(solution)/shard_map/pxy,qyz->pqxz/dot_general | solution.py:29
  36.3 0.1 broadcast_add_fusion.1
  36.3 0.1 and_and_fusion.1
  36.4 0.0 collective-permute-done.1
  36.4 28.5 %collective-permute-done = s32[3]{0:T(128)S(1)} collective-permute-done((s32[3]{0:T(128)}, s32[3]{0:T(128)S(1)}, u32[]{:S(2)}, u32[]{:S(2)}) %collective-permute-start) | collective-permute-done | bytes 44 | tf_op jit(solution)/shard_map/ppermute | solution.py:13
  64.9 0.1 and_and_fusion
  65.0 0.1 broadcast_add_fusion
  65.1 0.0 collective-permute-done.2
  65.1 0.0 collective-permute-done.3
  65.1 6.7 %fusion.7 = f32[3,256,3,256]{3,1,2,0:T(8,128)} fusion(f32[3,256,256]{2,1,0:T(8,128)} %collective-permute-done.2, f32[3,256,256]{2,1,0:T(8,128)} %collective-permute-done.3), kind=kOutput, calls=%fused_computation.6 | convolution fusion | flops 1811939328 | bytes 3932160 | tf_op jit(solution)/shard_map/pxy,qyz->pqxz/dot_general | solution.py:29
  71.8 0.0 copy-start
  71.8 4.6 %copy.11 = f32[3,256,3,256]{1,0,2,3:T(4,128)} copy(f32[3,256,3,256]{3,1,2,0:T(8,128)} %fusion.7) | data formatting | bytes 4718592 | tf_op jit(solution)/shard_map/pxy,qyz->pqxz/dot_general | solution.py:29
  76.4 0.0 copy-done
  76.4 5.1 %fusion = f32[6,256,256,1]{2,0,3,1:T(8,128)S(1)} fusion(f32[3,256,3,256]{1,0,2,3:T(4,128)} %copy.11, s32[3,3]{1,0:T(4,128)S(1)} %broadcast_add_fusion, s32[6]{0:T(128)S(1)} %bitcast.63, pred[3,3]{1,0:T(4,128)(4,1)S(1)} %and_and_fusion), kind=kOutput, calls=%fused_computation | convolution fusion | flops 42467436 | bytes 3932229 | tf_op jit(solution)/shard_map/fpq,pqxz->fxz/dot_general | solution.py:31
  81.5 3.3 %fusion.4 = f32[1,1,6,256,256]{4,2,3,1,0:T(8,128)S(1)} fusion(f32[6,256,256,1]{2,0,3,1:T(8,128)S(1)} %fusion, f32[3,256,3,256]{1,0,2,3:T(4,128)S(1)} %copy.8, s32[6]{0:T(128)S(1)} %bitcast.64, s32[3,3]{1,0:T(4,128)S(1)} %broadcast_add_fusion.1, pred[3,3]{1,0:T(4,128)(4,1)S(1)} %and_and_fusion.1), kind=kOutput, calls=%fused_computation.5 | convolution fusion | flops 42860652 | bytes 5505093 | tf_op jit(solution)/shard_map/fpq,pqxz->fxz/dot_general | solution.py:31
  84.7 1.6 %copy.6 = f32[1,1,6,256,256]{4,3,2,1,0:T(8,128)} copy(f32[1,1,6,256,256]{4,2,3,1,0:T(8,128)S(1)} %fusion.4) | data formatting | bytes 3145728 | tf_op jit(solution)/shard_map/broadcast_in_dim | solution.py:45
  (7 shorter events, 0.1 us)
Async XLA Ops:
  0.0 32.9 %copy-start.1 = (s32[1,1,3]{2,1,0:T(1,128)S(1)}, s32[1,1,3]{2,1,0:T(1,128)}, u32[]{:S(2)}) copy-start(s32[1,1,3]{2,1,0:T(1,128)} %param.8) | copy-start | bytes 40
  0.0 32.9 %copy-start.2 = (s32[1,1,3]{2,1,0:T(1,128)S(1)}, s32[1,1,3]{2,1,0:T(1,128)}, u32[]{:S(2)}) copy-start(s32[1,1,3]{2,1,0:T(1,128)} %param.6) | copy-start | bytes 40
  0.0 65.1 %collective-permute-start.2 = (f32[3,256,256]{2,1,0:T(8,128)}, f32[3,256,256]{2,1,0:T(8,128)}, u32[]{:S(2)}, u32[]{:S(2)}) collective-permute-start(f32[3,256,256]{2,1,0:T(8,128)} %bitcast.61), channel_id=1, source_target_pairs={{0,992},{32,0},{64,32},{96,64},{128,96},{160,128},{192,160},{224,1... | collective-permute-start | bytes 2359304 | tf_op jit(solution)/shard_map/ppermute | solution.py:13
  4.3 60.8 %collective-permute-start.3 = (f32[3,256,256]{2,1,0:T(8,128)}, f32[3,256,256]{2,1,0:T(8,128)}, u32[]{:S(2)}, u32[]{:S(2)}) collective-permute-start(f32[3,256,256]{2,1,0:T(8,128)} %bitcast.62), channel_id=1, source_target_pairs={{0,31},{1,0},{2,1},{3,2},{4,3},{5,4},{6,5},{7,6},{8,7},{9,8},{10,9... | collective-permute-start | bytes 2359304 | tf_op jit(solution)/shard_map/ppermute | solution.py:13
  7.2 29.2 %collective-permute-start.1 = (s32[3]{0:T(128)}, s32[3]{0:T(128)S(1)}, u32[]{:S(2)}, u32[]{:S(2)}) collective-permute-start(s32[3]{0:T(128)} %bitcast.65), channel_id=1, source_target_pairs={{0,992},{32,0},{64,32},{96,64},{128,96},{160,128},{192,160},{224,1... | collective-permute-start | bytes 44 | tf_op jit(solution)/shard_map/ppermute | solution.py:13
  10.2 54.7 %collective-permute-start = (s32[3]{0:T(128)}, s32[3]{0:T(128)S(1)}, u32[]{:S(2)}, u32[]{:S(2)}) collective-permute-start(s32[3]{0:T(128)} %bitcast.66), channel_id=1, source_target_pairs={{0,31},{1,0},{2,1},{3,2},{4,3},{5,4},{6,5},{7,6},{8,7},{9,8},{10,9... | collective-permute-start | bytes 44 | tf_op jit(solution)/shard_map/ppermute | solution.py:13
  71.8 4.6 %copy-start = (s32[1,1,6]{2,1,0:T(1,128)S(1)}, s32[1,1,6]{2,1,0:T(1,128)}, u32[]{:S(2)}) copy-start(s32[1,1,6]{2,1,0:T(1,128)} %param.9) | copy-start | bytes 76
where the time goes:
time: 86.8 us; the launch traced here: 86.4 us
  waiting for transfers between devices  28.5 us (33%)
  starting transfers between devices  26.2 us (30%)
  matrix products  21.6 us (25%)
  local copies, waits for them, and re-layouts  9.53 us (11%)
    ppermute x4, waiting for transfers between devices, passed_along(): lax.ppermute(array, axis, [(i, (i + by) % peers) for i in range(peers)])  28.5 us
    ppermute x4, starting transfers between devices, passed_along(): lax.ppermute(array, axis, [(i, (i + by) % peers) for i in range(peers)])  26.2 us
    dot_general x2, matrix products, pair_product(): jnp.einsum('pxy,qyz->pqxz', a_blocks, b_blocks, precision=lax.Precision.H...  13.3 us
    dot_general x2, matrix products, pair_product(): jnp.einsum('fpq,pqxz->fxz', select, prods, precision=lax.Precision.HIGHEST)  8.32 us
    dot_general x2, local copies, waits for them, and re-layouts, pair_product(): jnp.einsum('pxy,qyz->pqxz', a_blocks, b_blocks, precision=lax.Precision.H...  7.9 us
  transfers between devices with their start and end apart: 4, of which 1 were waited for; matrix products, arithmetic and copies ran while one was open for 12% of the time, Pallas kernels for 0%

commit v1 on v0

v1 whole, which is shorter than its diff:
```python
import jax
import jax.numpy as jnp
from jax import lax
from jax.experimental import pallas as pl
from jax.experimental.pallas import tpu as pltpu
from jax.sharding import PartitionSpec as P

BS = 256
SLOTS = 3
F = 6
ROWS = SLOTS * BS
LINES = 8
ZS = 16
DIRECT = 576
PIECE = ROWS // LINES
RELAYED = ROWS - DIRECT
SPREAD = True

MESH = pl.DeviceIdType.MESH
ANY = pl.BlockSpec(memory_space=pl.ANY)
SMEM = pl.BlockSpec(memory_space=pltpu.SMEM)


def exchange_kernel(a_ref, b_ref, ai_ref, bi_ref, a2_ref, b2_ref, ai2_ref, bi2_ref,
                    msg, relay, first, second, a_sems, i_sems, r_sems, b_sems, l_sems, f_sems, g_sems):
    row, col = lax.axis_index("row"), lax.axis_index("col")
    y, z_lo = lax.rem(row, LINES), lax.div(row, LINES)
    core, chip = lax.rem(col, 2), lax.div(col, 2)
    z_hi, x = lax.rem(chip, 4), lax.div(chip, 4)
    z = z_hi * 4 + z_lo

    def place(px, py, pz, pcore):
        pz = lax.rem(pz, ZS)
        return (lax.rem(pz, 4) * LINES + py, (lax.rem(px, 4) * 4 + lax.div(pz, 4)) * 2 + pcore)

    a_to, a_from = (row, lax.rem(col + 31, 32)), (row, lax.rem(col + 1, 32))
    b_to, b_from = (lax.rem(row + 31, 32), col), (lax.rem(row + 1, 32), col)
    relay_to, relay_from = place(x, y, z + 6, 0), place(x, y, z + 10, 0)
    origin_z = lax.rem(z + 10, ZS)
    relay_end = place(x + jnp.where(origin_z < 4, 3, 0), y, origin_z + 12, 1)
    relay_last = place(x + jnp.where(z_hi == 3, 1, 0), y, z + 10, 0)
    z_down, z_up = lax.rem(z_lo + 3, 4) * LINES, lax.rem(z_lo + 1, 4) * LINES
    here = z_lo * LINES

    barrier = pltpu.get_barrier_semaphore()

    def greet(device):
        pl.semaphore_signal(barrier, inc=1, device_id=device, device_id_type=MESH)

    greet(a_from)
    greet(b_from)

    @pl.when(core == 0)
    def _():
        greet(relay_from)

    @pl.when(core == 1)
    def _():
        greet(relay_last)

    @pl.when(y != 0)
    def _():
        greet((here, col))

    greet((z_up + y, col))

    @pl.when(y == LINES - 1)
    def _():
        for line in range(LINES - 1):
            greet((here + line, col))

    ints = (8, 128)
    lane = lax.broadcasted_iota(jnp.int32, ints, 1)
    for which, source in enumerate((ai_ref, bi_ref)):
        packed = jnp.zeros(ints, jnp.int32)
        for slot in range(SLOTS):
            packed = jnp.where(lane == slot, source[0, 0, slot], packed)
        msg[which] = packed

    dests = 3 + jnp.where(core == 0, 2, 0)
    dests = dests + jnp.where(y != LINES - 1, 1, 0) + jnp.where(y == 0, LINES - 1, 0)
    pl.semaphore_wait(barrier, dests)

    def remote(src, dst, sems, device):
        return pltpu.make_async_remote_copy(src_ref=src, dst_ref=dst, send_sem=sems.at[0], recv_sem=sems.at[1],
                                            device_id=device, device_id_type=MESH)

    head, tail = pl.ds(0, DIRECT), pl.ds(DIRECT, RELAYED)
    a_rest = remote(a_ref.at[tail], a2_ref.at[tail], a_sems.at[1], a_to)
    a_out = remote(a_ref.at[tail], relay, r_sems.at[0], relay_to)
    a_on = remote(relay, a2_ref.at[tail], a_sems.at[1], relay_end)
    a_main = remote(a_ref.at[head], a2_ref.at[head], a_sems.at[0], a_to)
    ints_a = remote(msg.at[0], ai2_ref, i_sems.at[0], a_to)
    ints_b = remote(msg.at[1], bi2_ref, i_sems.at[1], b_to)
    b_main = remote(b_ref, b2_ref, b_sems, b_to)

    @pl.when(core == 0)
    def _():
        a_out.start()

    @pl.when(core == 1)
    def _():
        a_rest.start()

    @pl.when(y != 0)
    def _():
        b_main.start()

    def part(line):
        return pl.ds(line * PIECE, PIECE)

    def first_leg(line):
        return pltpu.make_async_remote_copy(
            src_ref=b_ref.at[part(line)], dst_ref=first, send_sem=f_sems.at[line], recv_sem=l_sems.at[0],
            device_id=(here + line, col), device_id_type=MESH)

    lead_leg = remote(b_ref.at[part(0)], second, l_sems.at[pl.ds(1, 2)], (z_down, col))
    mid_leg = remote(first, second, l_sems.at[pl.ds(1, 2)], (z_down + y, col))
    end_leg = remote(first, b2_ref.at[part(LINES - 1)], l_sems.at[pl.ds(1, 2)], (z_down + y, col))
    my_part = pl.ds(pl.multiple_of(y * PIECE, PIECE), PIECE)
    last_leg = pltpu.make_async_remote_copy(
        src_ref=second, dst_ref=b2_ref.at[my_part], send_sem=l_sems.at[3], recv_sem=g_sems.at[y],
        device_id=(here + LINES - 1, col), device_id_type=MESH)

    @pl.when(y == 0)
    def _():
        lead_leg.start()
        for line in range(1, LINES):
            first_leg(line).start()

    a_main.start()
    ints_a.start()
    ints_b.start()

    @pl.when(y != 0)
    def _():
        first_leg(1).wait_recv()

    @pl.when((y != 0) & (y != LINES - 1))
    def _():
        mid_leg.start()

    @pl.when(y == LINES - 1)
    def _():
        end_leg.start()

    @pl.when(y != LINES - 1)
    def _():
        mid_leg.wait_recv()
        last_leg.start()

    @pl.when(core == 0)
    def _():
        a_out.wait_recv()
        a_on.start()

    mid_leg.wait_send()

    @pl.when(y == LINES - 1)
    def _():
        end_leg.wait_recv()
        for line in range(LINES - 1):
            pltpu.make_async_remote_copy(
                src_ref=second, dst_ref=b2_ref.at[part(line)], send_sem=l_sems.at[3], recv_sem=g_sems.at[line],
                device_id=(here + LINES - 1, col), device_id_type=MESH).wait_recv()

    @pl.when(y != LINES - 1)
    def _():
        last_leg.wait_send()
        b_main.wait_recv()

    @pl.when(y != 0)
    def _():
        b_main.wait_send()

    @pl.when(y == 0)
    def _():
        for line in range(1, LINES):
            first_leg(line).wait_send()

    ints_a.wait()
    ints_b.wait()
    a_main.wait()

    @pl.when(core == 0)
    def _():
        a_out.wait_send()

    a_rest.wait()


def exchange(a, b, a_index, b_index):
    panel = jax.ShapeDtypeStruct((ROWS, BS), jnp.float32)
    ints = jax.ShapeDtypeStruct((8, 128), jnp.int32)
    dma = pltpu.SemaphoreType.DMA
    return pl.pallas_call(
        exchange_kernel,
        out_shape=(panel, panel, ints, ints),
        in_specs=[ANY, ANY, SMEM, SMEM],
        out_specs=(ANY, ANY, ANY, ANY),
        scratch_shapes=[
            pltpu.VMEM((2, 8, 128), jnp.int32),
            pltpu.VMEM((RELAYED, BS), jnp.float32),
            pltpu.VMEM((PIECE, BS), jnp.float32),
            pltpu.VMEM((PIECE, BS), jnp.float32),
            dma((2, 2)),
            dma((2, 2)),
            dma((1, 2)),
            dma((2,)),
            dma((4,)),
            dma((LINES,)),
            dma((LINES,)),
        ],
        compiler_params=pltpu.CompilerParams(collective_id=0, has_side_effects=True),
        cost_estimate=pl.CostEstimate(flops=0, bytes_accessed=4 * ROWS * BS * 4, transcendentals=0),
        name="exchange",
    )(a, b, a_index, b_index)


def product_kernel(a0, b0, a1, b1, ai0, bi0, ai1, bi1, ci, out, va, vb, acc, plan, a_sem, b_sem, out_sem):
    need_a = [jnp.int32(0)] * (2 * SLOTS)
    need_b = [jnp.int32(0)] * (2 * SLOTS)
    count = jnp.int32(0)
    touched = [jnp.int32(0)] * F
    kept = [ci[0, 0, f] for f in range(F)]
    steps = (
        ([ai0[0, 0, p] for p in range(SLOTS)], [bi0[0, 0, q] for q in range(SLOTS)]),
        ([ai1[0, p] for p in range(SLOTS)], [bi1[0, q] for q in range(SLOTS)]),
    )
    for step, (a_slots, b_slots) in enumerate(steps):
        for p, v in enumerate(a_slots):
            for q, w in enumerate(b_slots):
                meet = (v < 16) & (w < 16) & ((v & 3) == (w >> 2))
                target = (v & 12) + (w & 3)
                place = jnp.int32(0)
                hit = jnp.int32(0)
                for f in range(F):
                    mine = (meet & (kept[f] == target)).astype(jnp.int32)
                    place = place + f * mine
                    hit = hit + mine
                    touched[f] = touched[f] | mine
                plan[count] = ((step * SLOTS + p) * 8 + step * SLOTS + q) * 8 + place
                count = count + hit
                need_a[step * SLOTS + p] |= hit
                need_b[step * SLOTS + q] |= hit

    def fetches():
        for step, (a, b) in enumerate(((a0, b0), (a1, b1))):
            for p in range(SLOTS):
                n = step * SLOTS + p
                part = pl.ds(p * BS, BS)
                yield need_a[n], pltpu.make_async_copy(a.at[part], va.at[n], a_sem.at[n])
                yield need_b[n], pltpu.make_async_copy(b.at[part], vb.at[n], b_sem.at[n])

    for need, copy in fetches():
        pl.when(need != 0)(copy.start)

    writes = [pltpu.make_async_copy(acc.at[f], out.at[f], out_sem.at[f]) for f in range(F)]
    for f in range(F):
        acc[f] = jnp.zeros((BS, BS), jnp.float32)
        pl.when(touched[f] == 0)(writes[f].start)

    for need, copy in fetches():
        pl.when(need != 0)(copy.wait)

    def pair(t, carry):
        entry = plan[t]
        a, b = va[entry >> 6], vb[(entry >> 3) & 7]
        f = entry & 7
        a_hi, b_hi = a.astype(jnp.bfloat16), b.astype(jnp.bfloat16)
        a_lo = (a - a_hi.astype(jnp.float32)).astype(jnp.bfloat16)
        b_lo = (b - b_hi.astype(jnp.float32)).astype(jnp.bfloat16)

        def dot(left, right):
            return jnp.dot(left, right, preferred_element_type=jnp.float32)

        acc[f] += dot(a_hi, b_hi) + (dot(a_hi, b_lo) + dot(a_lo, b_hi))
        return carry

    lax.fori_loop(0, count, pair, 0)
    for f in range(F):
        pl.when(touched[f] != 0)(writes[f].start)
    for f in range(F):
        writes[f].wait()


def products(a0, b0, a1, b1, ai0, bi0, ai1, bi1, ci):
    dma = pltpu.SemaphoreType.DMA
    return pl.pallas_call(
        product_kernel,
        out_shape=jax.ShapeDtypeStruct((F, BS, BS), jnp.float32),
        in_specs=[ANY] * 4 + [SMEM] * 5,
        out_specs=ANY,
        scratch_shapes=[
            pltpu.VMEM((2 * SLOTS, BS, BS), jnp.float32),
            pltpu.VMEM((2 * SLOTS, BS, BS), jnp.float32),
            pltpu.VMEM((F, BS, BS), jnp.float32),
            pltpu.SMEM((128,), jnp.int32),
            dma((2 * SLOTS,)),
            dma((2 * SLOTS,)),
            dma((F,)),
        ],
        compiler_params=pltpu.CompilerParams(vmem_limit_bytes=16 * 1024 * 1024),
        cost_estimate=pl.CostEstimate(flops=6 * BS ** 3, bytes_accessed=12 * BS * BS * 4, transcendentals=0),
        name="products",
    )(a0, b0, a1, b1, ai0, bi0, ai1, bi1, ci)


def per_device(a_panels, a_index, b_panels, b_index, c_index):
    a0 = a_panels.reshape(ROWS, BS)
    b0 = b_panels.reshape(ROWS, BS)
    a1, b1, ai1, bi1 = exchange(a0, b0, a_index, b_index)
    blocks = products(a0, b0, a1, b1, a_index, b_index, ai1, bi1, c_index)
    return blocks[None, None]


def solution(mesh):
    return jax.shard_map(
        per_device,
        mesh=mesh,
        in_specs=(
            P("row", "col", None, None, None),
            P("row", "col", None),
            P("row", "col", None, None, None),
            P("row", "col", None),
            P("row", "col", None),
        ),
        out_specs=P("row", "col", None, None, None),
        check_vma=False,
    )
```

time: 86.8 us -> 70.5 us (0.81)
  the two profiles are of different devices: /device:TPU:199 before, /device:TPU:13 now
where the time goes in v1:
time: 70.5 us; the launch traced here: 70.2 us
  Pallas kernels  66.5 us (94%)
  local copies, waits for them, and re-layouts  3.63 us (5%)
    pallas_call x1, Pallas kernels, exchange(): pl.pallas_call(exchange_kernel, out_shape=(panel, panel, ints, ints), in_...  64 us
    unnamed x18, local copies, waits for them, and re-layouts  3.63 us
    pallas_call x1, Pallas kernels, products(): pl.pallas_call(product_kernel, out_shape=jax.ShapeDtypeStruct((F, BS, BS)...  2.5 us

profile of v1, /device:TPU:13, one launch (start us, length us, event | category | flops | bytes accessed | tf_op | source)
XLA Modules:
  0.0 70.2 jit_solution(17847939164515788087)
XLA Ops:
  0.0 0.0 copy-start.7
  0.0 0.0 copy-start.6
  0.0 0.0 copy-start.8
  0.0 0.0 copy-start.1
  0.0 0.0 copy-start
  0.0 64.0 %exchange.1 = (f32[768,256]{1,0:T(8,128)}, f32[768,256]{1,0:T(8,128)}, s32[8,128]{1,0:T(8,128)}, s32[8,128]{1,0:T(8,128)}) custom-call(f32[768,256]{1,0:T(8,128)} %bitcast.3, f32[768,256]{1,0:T(8,128)} %bitcast.5, s32[1,1,3]{2,1,0:T(1,128)} %ai0.1, s32[1,1,3]{2,1,0:T(1,128)} %bi0.1), custom_call_target="tpu_custom_call" | custom-call | bytes 3145728 | tf_op jit(solution)/shard_map/exchange/pallas_call | solution.py:196
  64.0 0.0 copy-done.7
  64.0 0.0 copy-done.6
  64.1 0.0 copy-done.8
  64.1 0.0 copy-done.1
  64.1 0.0 copy-done
  64.1 0.0 copy-start.2
  64.1 1.1 %copy-done.2 = f32[768,256]{1,0:T(8,128)S(1)} copy-done((f32[768,256]{1,0:T(8,128)S(1)}, f32[768,256]{1,0:T(8,128)}, u32[]{:S(2)}) %copy-start.2) | copy-done | bytes 786456
  65.2 0.0 copy-start.3
  65.2 1.1 %copy-done.3 = f32[768,256]{1,0:T(8,128)S(1)} copy-done((f32[768,256]{1,0:T(8,128)S(1)}, f32[768,256]{1,0:T(8,128)}, u32[]{:S(2)}) %copy-start.3) | copy-done | bytes 786456
  66.4 0.0 copy-start.4
  66.4 0.7 copy-done.4
  67.0 0.0 copy-start.5
  67.0 0.7 copy-done.5
  67.7 2.5 %products.1 = f32[6,256,256]{2,1,0:T(8,128)} custom-call(f32[768,256]{1,0:T(8,128)S(1)} %bitcast.4, f32[768,256]{1,0:T(8,128)S(1)} %bitcast.6, f32[768,256]{1,0:T(8,128)S(1)} %copy-done.2, f32[768,256]{1,0:T(8,128)S(1)} %copy-done.3, s32[1,1,3]{2,1,0:T(1,128)S(1)} %copy-done.6, s32[1,1,3]{2,1,0:T(1,128)S(1)} %copy-done.7, s32[8,128]{1,0:T(8,128)S(1)} %copy-done.4, ...), custom_call_target="tpu_custom_call" | custom-call | flops 100663296 | bytes 3145728 | tf_op jit(solution)/shard_map/products/pallas_call | solution.py:289
Async XLA Ops:
  0.0 64.0 %copy-start.7 = (s32[1,1,3]{2,1,0:T(1,128)S(1)}, s32[1,1,3]{2,1,0:T(1,128)}, u32[]{:S(2)}) copy-start(s32[1,1,3]{2,1,0:T(1,128)} %bi0.1) | copy-start | bytes 40
  0.0 64.0 %copy-start.6 = (s32[1,1,3]{2,1,0:T(1,128)S(1)}, s32[1,1,3]{2,1,0:T(1,128)}, u32[]{:S(2)}) copy-start(s32[1,1,3]{2,1,0:T(1,128)} %ai0.1) | copy-start | bytes 40
  0.0 64.1 %copy-start.8 = (s32[1,1,6]{2,1,0:T(1,128)S(1)}, s32[1,1,6]{2,1,0:T(1,128)}, u32[]{:S(2)}) copy-start(s32[1,1,6]{2,1,0:T(1,128)} %ci.1) | copy-start | bytes 76
  0.0 64.1 %copy-start.1 = (f32[1,1,3,256,256]{4,3,2,1,0:T(8,128)S(1)}, f32[1,1,3,256,256]{4,3,2,1,0:T(8,128)}, u32[]{:S(2)}) copy-start(f32[1,1,3,256,256]{4,3,2,1,0:T(8,128)} %param.7) | copy-start | bytes 2359300
  0.0 64.1 %copy-start = (f32[1,1,3,256,256]{4,3,2,1,0:T(8,128)S(1)}, f32[1,1,3,256,256]{4,3,2,1,0:T(8,128)}, u32[]{:S(2)}) copy-start(f32[1,1,3,256,256]{4,3,2,1,0:T(8,128)} %param.5) | copy-start | bytes 2359300
  64.1 1.1 %copy-start.2 = (f32[768,256]{1,0:T(8,128)S(1)}, f32[768,256]{1,0:T(8,128)}, u32[]{:S(2)}) copy-start(f32[768,256]{1,0:T(8,128)} %get-tuple-element.9.a1) | copy-start | bytes 2359300
  65.2 1.1 %copy-start.3 = (f32[768,256]{1,0:T(8,128)S(1)}, f32[768,256]{1,0:T(8,128)}, u32[]{:S(2)}) copy-start(f32[768,256]{1,0:T(8,128)} %get-tuple-element.10.b1) | copy-start | bytes 2359300
  66.4 0.7 copy-start.4
  67.0 0.7 copy-start.5

commit v2 on v1

v2 whole, which is shorter than its diff:
```python
import jax
import jax.numpy as jnp
from jax import lax
from jax.experimental import pallas as pl
from jax.experimental.pallas import tpu as pltpu
from jax.sharding import PartitionSpec as P

BS = 256
SLOTS = 3
F = 6
ROWS = SLOTS * BS
LINES = 8
ZS = 16
CHUNK = 96
SHARE = (4, 0, 2, 0)
MOST = max(1, max(SHARE))
UP = 5
PIECE = ROWS // LINES
VMEM = 60 * 1024 * 1024

MESH = pl.DeviceIdType.MESH
ANY = pl.BlockSpec(memory_space=pl.ANY)
HBM = pl.BlockSpec(memory_space=pltpu.HBM)
SMEM = pl.BlockSpec(memory_space=pltpu.SMEM)


def exchange_kernel(a_ref, b_ref, ai_ref, bi_ref, a2_ref, b2_ref, i2_ref, msg, relay, first, second,
                    a_sems, i_sems, up_send, up_recv, on_send, on_recv, b_sems, f_sems, s_sems, h_sems, m_sems, t_sems, g_sems,
                    ready):
    row, col = lax.axis_index("row"), lax.axis_index("col")
    y, z_lo = lax.rem(row, LINES), lax.div(row, LINES)
    core, chip = lax.rem(col, 2), lax.div(col, 2)
    z_hi, x = lax.rem(chip, 4), lax.div(chip, 4)
    z = z_hi * 4 + z_lo
    core0, core1 = core == 0, core == 1

    def place(px, py, pz, pcore):
        pz = lax.rem(pz, ZS)
        return (lax.rem(pz, 4) * LINES + py, (lax.rem(px, 4) * 4 + lax.div(pz, 4)) * 2 + pcore)

    def when(*conditions):
        whole = conditions[0]
        for condition in conditions[1:]:
            whole = whole & condition
        return pl.when(whole)

    def one(*conditions):
        whole = conditions[0]
        for condition in conditions[1:]:
            whole = whole & condition
        return jnp.where(whole, 1, 0)

    a_to, a_from = (row, lax.rem(col + 31, 32)), (row, lax.rem(col + 1, 32))
    relay_to = place(x, y, z + UP, 0)
    sender_z = lax.rem(z + ZS - UP, ZS)
    sender_hi = lax.div(sender_z, 4)
    sender = place(x, y, z + ZS - UP, 0)
    relay_end = place(x + jnp.where(sender_hi == 0, 3, 0), y, sender_z + 12, 1)
    last_relay = place(x + jnp.where(z_hi == 3, 1, 0), y, z + 4 + UP, 0)
    from_hi = lax.rem(z_hi + 1, 4)

    def relayed(group):
        found = group < 0
        for g in range(4):
            if SHARE[g]:
                found = found | (group == g)
        return found

    sends_up, relays, gets_up = core0 & relayed(z_hi), core0 & relayed(sender_hi), core1 & relayed(from_hi)
    up_late = z + UP < ZS
    in_late = z >= UP
    on_late = z < ZS - 4 - UP + 2
    got_late = z >= 12 - UP
    down_late, end_late = z_hi == 0, z_hi == 3

    z_down, z_up = lax.rem(z_lo + 3, 4) * LINES, lax.rem(z_lo + 1, 4) * LINES
    here = z_lo * LINES
    top, bottom = y == 0, y == LINES - 1
    b_to = (lax.rem(row + 31, 32), col)
    b_from = (lax.rem(row + 1, 32), col)
    col0, col1 = col - core, col - core + 1

    barrier = pltpu.get_barrier_semaphore()

    def greet(device):
        pl.semaphore_signal(barrier, inc=1, device_id=device, device_id_type=MESH)

    @when(~bottom)
    def _():
        greet(b_from)

    @when(core0)
    def _():
        greet(a_from)

    @when(core1, ~end_late)
    def _():
        greet(a_from)

    @when(core0, down_late)
    def _():
        greet(a_to)

    @when(sends_up, up_late)
    def _():
        greet(relay_to)

    @when(relays, ~in_late)
    def _():
        greet(sender)

    @when(relays, on_late)
    def _():
        greet(relay_end)

    @when(gets_up, ~got_late)
    def _():
        greet(last_relay)

    @when(top)
    def _():
        for line in range(1, LINES):
            greet((here + line, col1))
        greet((z_down, col1))
        greet(b_to)

    @when(core1, ~top, ~bottom)
    def _():
        greet((z_up + y, col1))

    @when(bottom)
    def _():
        for line in range(LINES - 1):
            greet((here + line, col1))
        greet((z_up + LINES - 1, col1))

    ints = (8, 128)
    lane = lax.broadcasted_iota(jnp.int32, ints, 1)
    for which, source in enumerate((ai_ref, bi_ref)):
        packed = jnp.zeros(ints, jnp.int32)
        for slot in range(SLOTS):
            packed = jnp.where(lane == slot, source[0, 0, slot], packed)
        msg[which] = packed

    greetings = one(~top) + one(core1) + one(core0, ~down_late) + one(core1, end_late)
    greetings = greetings + one(sends_up, ~up_late) + one(relays, in_late) + one(relays, ~on_late)
    greetings = greetings + one(gets_up, got_late) + 4 * one(core1) + one(core1, ~top, ~bottom)
    greetings = greetings + one(bottom)
    @when(greetings > 0)
    def _():
        pl.semaphore_wait(barrier, greetings)

    def tell(which, device):
        pl.semaphore_signal(ready.at[which], inc=1, device_id=device, device_id_type=MESH)

    @when(core1, end_late)
    def _():
        tell(0, a_from)

    @when(core1, ~top)
    def _():
        tell(3, (here, col0))
        tell(3, (here, col1))

    @when(core1, top)
    def _():
        tell(3, (z_up, col0))
        tell(3, (z_up, col1))

    @when(bottom)
    def _():
        tell(3, b_from)

    @when(relays, in_late)
    def _():
        tell(1, sender)

    @when(gets_up, got_late)
    def _():
        tell(2, last_relay)

    def remote(src, dst, send, recv, device):
        return pltpu.make_async_remote_copy(src_ref=src, dst_ref=dst, send_sem=send, recv_sem=recv,
                                            device_id=device, device_id_type=MESH)

    def head(g):
        rows = pl.ds(0, ROWS - SHARE[g] * CHUNK)
        return remote(a_ref.at[rows], a2_ref.at[rows], a_sems.at[0], a_sems.at[1], a_to)

    def chunk_rows(g, n):
        return pl.ds(ROWS - SHARE[g] * CHUNK + n * CHUNK, CHUNK)

    def slot_rows(n):
        return pl.ds(n * CHUNK, CHUNK)

    def up(g, n):
        return remote(a_ref.at[chunk_rows(g, n)], relay.at[slot_rows(n)], up_send.at[n], up_recv.at[n], relay_to)

    def on(g, n):
        return remote(relay.at[slot_rows(n)], a2_ref.at[chunk_rows(g, n)], on_send.at[n], on_recv.at[n], relay_end)

    whole = remote(a_ref, a2_ref, a_sems.at[0], a_sems.at[1], a_to)
    ints_a = remote(msg.at[0], i2_ref.at[0], i_sems.at[0], i_sems.at[1], a_to)
    ints_b = remote(msg.at[1], i2_ref.at[1], i_sems.at[2], i_sems.at[3], b_to)
    b_main = remote(b_ref, b2_ref, b_sems.at[0], b_sems.at[1], b_to)

    def part(line):
        return pl.ds(line * PIECE, PIECE)

    my_part = pl.ds(pl.multiple_of(y * PIECE, PIECE), PIECE)

    def leg_y(line, c):
        return remote(b_ref.at[part(line)], first.at[c], f_sems.at[line], h_sems.at[c], (here + line, col1))

    def leg_z(c):
        return remote(b_ref.at[part(0)], second.at[c], f_sems.at[0], s_sems.at[c], (z_down, col1))

    def then_z(c):
        return remote(first.at[c], second.at[c], m_sems.at[c], s_sems.at[c], (z_down + y, col1))

    def then_end(c):
        return remote(first.at[c], b2_ref.at[part(LINES - 1)], m_sems.at[c], g_sems.at[LINES - 1],
                      (z_down + LINES - 1, col0 + c))

    def then_y(c):
        return remote(second.at[c], b2_ref.at[my_part], t_sems.at[c], g_sems.at[y], (here + LINES - 1, col0 + c))

    def arrival(line):
        return remote(second.at[0], b2_ref.at[part(line)], t_sems.at[0], g_sems.at[line], (here, col))

    @when(core1)
    def _():
        whole.start()

    @when(~top)
    def _():
        b_main.start()
        ints_b.start()

    @when(core1)
    def _():
        ints_a.start()

    for g in range(1, 4):
        @when(core0, z_hi == g)
        def _():
            ints_a.start()
            head(g).start()

    for c in range(2):
        @when(top, core == c)
        def _():
            pl.semaphore_wait(ready.at[3], LINES + 1)
            for line in (4, 3, 5, 2, 6, 1, 7):
                leg_y(line, c).start()
            leg_z(c).start()
            ints_b.start()

    for g in range(4):
        if SHARE[g]:
            @when(core0, z_hi == g)
            def _():
                @when(up_late)
                def _():
                    pl.semaphore_wait(ready.at[1], 1)

                for n in range(SHARE[g]):
                    up(g, n).start()

    @when(core0, down_late)
    def _():
        pl.semaphore_wait(ready.at[0], 1)
        ints_a.start()
        head(0).start()

    for g in range(4):
        if SHARE[g]:
            @when(core0, sender_hi == g)
            def _():
                @when(on_late)
                def _():
                    pl.semaphore_wait(ready.at[2], 1)

                for n in range(SHARE[g]):
                    up(g, n).wait_recv()
                    on(g, n).start()

    for c in range(2):
        @when(core1, ~top)
        def _():
            leg_y(1, c).wait_recv()

        @when(core1, ~top, ~bottom)
        def _():
            then_z(c).start()

        @when(core1, bottom)
        def _():
            then_end(c).start()

    for c in range(2):
        @when(core1, ~bottom)
        def _():
            leg_z(c).wait_recv()
            then_y(c).start()

    ints_a.wait()
    ints_b.wait()

    @when(core1)
    def _():
        whole.wait_send()

    @when(core0)
    def _():
        whole.wait_recv()

    @when(~top)
    def _():
        b_main.wait_send()

    @when(~bottom)
    def _():
        b_main.wait_recv()

    @when(top)
    def _():
        leg_z(0).wait_send()
        for line in range(1, LINES):
            leg_y(line, 0).wait_send()

    for c in range(2):
        @when(core1, ~top)
        def _():
            then_z(c).wait_send()

        @when(core1, ~bottom)
        def _():
            then_y(c).wait_send()

    @when(bottom)
    def _():
        for line in range(LINES):
            arrival(line).wait_recv()

    for g in range(4):
        @when(core0, z_hi == g)
        def _():
            for n in range(SHARE[g]):
                up(g, n).wait_send()
            head(g).wait_send()

        @when(core0, sender_hi == g)
        def _():
            for n in range(SHARE[g]):
                on(g, n).wait_send()

        @when(core1, from_hi == g)
        def _():
            head(g).wait_recv()
            for n in range(SHARE[g]):
                on(g, n).wait_recv()


def exchange(a, b, a_index, b_index):
    panel = jax.ShapeDtypeStruct((ROWS, BS), jnp.float32)
    ints = jax.ShapeDtypeStruct((2, 8, 128), jnp.int32)
    dma = pltpu.SemaphoreType.DMA
    return pl.pallas_call(
        exchange_kernel,
        out_shape=(panel, panel, ints),
        in_specs=[HBM, HBM, SMEM, SMEM],
        out_specs=(HBM, HBM, HBM),
        scratch_shapes=[
            pltpu.VMEM((2, 8, 128), jnp.int32),
            pltpu.VMEM((MOST * CHUNK, BS), jnp.float32),
            pltpu.VMEM((2, PIECE, BS), jnp.float32),
            pltpu.VMEM((2, PIECE, BS), jnp.float32),
            dma((2,)),
            dma((4,)),
            dma((MOST,)),
            dma((MOST,)),
            dma((MOST,)),
            dma((MOST,)),
            dma((2,)),
            dma((LINES,)),
            dma((2,)),
            dma((2,)),
            dma((2,)),
            dma((2,)),
            dma((LINES,)),
            pltpu.SemaphoreType.REGULAR((4,)),
        ],
        compiler_params=pltpu.CompilerParams(collective_id=0, has_side_effects=True, vmem_limit_bytes=VMEM),
        cost_estimate=pl.CostEstimate(flops=0, bytes_accessed=4 * ROWS * BS * 4, transcendentals=0),
        name="exchange",
    )(a, b, a_index, b_index)


def product_kernel(a0, b0, a1, b1, ai0, bi0, i1, ci, out, va, vb, acc, later, plan, a_sem, b_sem, out_sem, i_sem):
    fetch = pltpu.make_async_copy(i1, later, i_sem)
    fetch.start()
    for f in range(F):
        acc[f] = jnp.zeros((BS, BS), jnp.float32)
    fetch.wait()
    need_a = [jnp.int32(0)] * (2 * SLOTS)
    need_b = [jnp.int32(0)] * (2 * SLOTS)
    count = jnp.int32(0)
    touched = [jnp.int32(0)] * F
    kept = [ci[0, 0, f] for f in range(F)]
    steps = (
        ([ai0[0, 0, p] for p in range(SLOTS)], [bi0[0, 0, q] for q in range(SLOTS)]),
        ([later[0, 0, p] for p in range(SLOTS)], [later[1, 0, q] for q in range(SLOTS)]),
    )
    for step, (a_slots, b_slots) in enumerate(steps):
        for p, v in enumerate(a_slots):
            for q, w in enumerate(b_slots):
                meet = (v < 16) & (w < 16) & ((v & 3) == (w >> 2))
                target = (v & 12) + (w & 3)
                place = jnp.int32(0)
                hit = jnp.int32(0)
                for f in range(F):
                    mine = (meet & (kept[f] == target)).astype(jnp.int32)
                    place = place + f * mine
                    hit = hit + mine
                    touched[f] = touched[f] | mine
                plan[count] = ((step * SLOTS + p) * 8 + step * SLOTS + q) * 8 + place
                count = count + hit
                need_a[step * SLOTS + p] |= hit
                need_b[step * SLOTS + q] |= hit

    def fetches():
        for step, (a, b) in enumerate(((a0, b0), (a1, b1))):
            for p in range(SLOTS):
                n = step * SLOTS + p
                part = pl.ds(p * BS, BS)
                yield need_a[n], pltpu.make_async_copy(a.at[part], va.at[n], a_sem.at[n])
                yield need_b[n], pltpu.make_async_copy(b.at[part], vb.at[n], b_sem.at[n])

    for need, copy in fetches():
        pl.when(need != 0)(copy.start)

    writes = [pltpu.make_async_copy(acc.at[f], out.at[f], out_sem.at[f]) for f in range(F)]
    for f in range(F):
        pl.when(touched[f] == 0)(writes[f].start)

    for need, copy in fetches():
        pl.when(need != 0)(copy.wait)

    def pair(t, carry):
        entry = plan[t]
        a, b = va[entry >> 6], vb[(entry >> 3) & 7]
        f = entry & 7
        a_hi, b_hi = a.astype(jnp.bfloat16), b.astype(jnp.bfloat16)
        a_lo = (a - a_hi.astype(jnp.float32)).astype(jnp.bfloat16)
        b_lo = (b - b_hi.astype(jnp.float32)).astype(jnp.bfloat16)

        def dot(left, right):
            return jnp.dot(left, right, preferred_element_type=jnp.float32)

        acc[f] += dot(a_hi, b_hi) + (dot(a_hi, b_lo) + dot(a_lo, b_hi))
        return carry

    lax.fori_loop(0, count, pair, 0)
    for f in range(F):
        pl.when(touched[f] != 0)(writes[f].start)
    for f in range(F):
        writes[f].wait()


def products(a0, b0, a1, b1, ai0, bi0, i1, ci):
    dma = pltpu.SemaphoreType.DMA
    return pl.pallas_call(
        product_kernel,
        out_shape=jax.ShapeDtypeStruct((F, BS, BS), jnp.float32),
        in_specs=[ANY, ANY, HBM, HBM, SMEM, SMEM, HBM, SMEM],
        out_specs=ANY,
        scratch_shapes=[
            pltpu.VMEM((2 * SLOTS, BS, BS), jnp.float32),
            pltpu.VMEM((2 * SLOTS, BS, BS), jnp.float32),
            pltpu.VMEM((F, BS, BS), jnp.float32),
            pltpu.SMEM((2, 8, 128), jnp.int32),
            pltpu.SMEM((128,), jnp.int32),
            dma((2 * SLOTS,)),
            dma((2 * SLOTS,)),
            dma((F,)),
            dma,
        ],
        compiler_params=pltpu.CompilerParams(vmem_limit_bytes=VMEM),
        cost_estimate=pl.CostEstimate(flops=6 * BS ** 3, bytes_accessed=12 * BS * BS * 4, transcendentals=0),
        name="products",
    )(a0, b0, a1, b1, ai0, bi0, i1, ci)


def per_device(a_panels, a_index, b_panels, b_index, c_index):
    a0 = a_panels.reshape(ROWS, BS)
    b0 = b_panels.reshape(ROWS, BS)
    a1, b1, i1 = exchange(a0, b0, a_index, b_index)
    blocks = products(a0, b0, a1, b1, a_index, b_index, i1, c_index)
    return blocks[None, None]


def solution(mesh):
    return jax.shard_map(
        per_device,
        mesh=mesh,
        in_specs=(
            P("row", "col", None, None, None),
            P("row", "col", None),
            P("row", "col", None, None, None),
            P("row", "col", None),
            P("row", "col", None),
        ),
        out_specs=P("row", "col", None, None, None),
        check_vma=False,
    )
```

time: 70.5 us -> 53.1 us (0.75)
  the two profiles are of different devices: /device:TPU:13 before, /device:TPU:119 now
where the time goes in v2:
time: 53.1 us; the launch traced here: 52.8 us
  Pallas kernels  52.8 us (99%)
    pallas_call x1, Pallas kernels, exchange(): pl.pallas_call(exchange_kernel, out_shape=(panel, panel, ints), in_specs=...  48 us
    pallas_call x1, Pallas kernels, products(): pl.pallas_call(product_kernel, out_shape=jax.ShapeDtypeStruct((F, BS, BS)...  4.87 us

profile of v2, /device:TPU:119, one launch (start us, length us, event | category | flops | bytes accessed | tf_op | source)
XLA Modules:
  0.0 52.8 jit_solution(13776309125499219207)
XLA Ops:
  0.0 48.0 %exchange.1 = (f32[768,256]{1,0:T(8,128)}, f32[768,256]{1,0:T(8,128)}, s32[2,8,128]{2,1,0:T(8,128)}) custom-call(f32[768,256]{1,0:T(8,128)} %bitcast.3, f32[768,256]{1,0:T(8,128)} %bitcast.5, s32[1,1,3]{2,1,0:T(1,128)} %ai0.1, s32[1,1,3]{2,1,0:T(1,128)} %bi0.1), custom_call_target="tpu_custom_call" | custom-call | bytes 3145728 | tf_op jit(solution)/shard_map/exchange/pallas_call | solution.py:369
  48.0 4.9 %products.1 = f32[6,256,256]{2,1,0:T(8,128)} custom-call(f32[768,256]{1,0:T(8,128)} %bitcast.4, f32[768,256]{1,0:T(8,128)} %bitcast.6, f32[768,256]{1,0:T(8,128)} %get-tuple-element.8.a1, f32[768,256]{1,0:T(8,128)} %get-tuple-element.9.b1, s32[1,1,3]{2,1,0:T(1,128)} %ai0.1, s32[1,1,3]{2,1,0:T(1,128)} %bi0.1, s32[2,8,128]{2,1,0:T(8,128)} %get-tuple-element.10.i1, ...), custom_call_target="tpu_custom_call" | custom-call | flops 100663296 | bytes 3145728 | tf_op jit(solution)/shard_map/products/pallas_call | solution.py:473

commit v3 on v2

v3 whole, which is shorter than its diff:
```python
import jax
import jax.numpy as jnp
from jax import lax
from jax.experimental import pallas as pl
from jax.experimental.pallas import tpu as pltpu
from jax.sharding import PartitionSpec as P

BS = 256
SLOTS = 3
F = 6
ROWS = SLOTS * BS
LINES = 8
ZS = 16
CHUNK = 96
SHARE = (4, 4, 4, 4, 0, 0, 0, 2, 2, 2, 0, 2, 0, 0, 0, 0)
COUNTS = sorted(set(SHARE))
TURNS = False
FIRST = False
MOST = max(1, max(SHARE))
UP = 5
PIECE = ROWS // LINES
VMEM = 60 * 1024 * 1024

NEED_A = SLOTS * SLOTS
NEED_B = NEED_A + SLOTS
TOUCHED = NEED_B + SLOTS
BEGUN = TOUCHED + F
PLAN = BEGUN + F
HALF = F // 2

MESH = pl.DeviceIdType.MESH
HBM = pl.BlockSpec(memory_space=pltpu.HBM)
SMEM = pl.BlockSpec(memory_space=pltpu.SMEM)


def block_product(a, b):
    a_hi, b_hi = a.astype(jnp.bfloat16), b.astype(jnp.bfloat16)
    a_lo = (a - a_hi.astype(jnp.float32)).astype(jnp.bfloat16)
    b_lo = (b - b_hi.astype(jnp.float32)).astype(jnp.bfloat16)

    def dot(left, right):
        return jnp.dot(left, right, preferred_element_type=jnp.float32)

    return dot(a_hi, b_hi) + (dot(a_hi, b_lo) + dot(a_lo, b_hi))


def plan_later(slots, kept, plan):
    need_b = [jnp.int32(0)] * SLOTS
    touched = [jnp.int32(0)] * F
    for p in range(SLOTS):
        v = slots[0, 0, p]
        need_a = jnp.int32(0)
        for q in range(SLOTS):
            w = slots[1, 0, q]
            target = jnp.where((v < 16) & (w < 16) & ((v & 3) == (w >> 2)), (v & 12) + (w & 3), -1)
            place = jnp.int32(F)
            for f in range(F):
                mine = kept[0, 0, f] == target
                place = jnp.where(mine, f, place)
                touched[f] = jnp.where(mine, 1, touched[f])
            hit = jnp.where(place < F, 1, 0)
            plan[p * SLOTS + q] = place
            need_a = need_a | hit
            need_b[q] = need_b[q] | hit
        plan[NEED_A + p] = need_a
    for q in range(SLOTS):
        plan[NEED_B + q] = need_b[q]
    for f in range(F):
        plan[TOUCHED + f] = touched[f]


def wanted_slot(f, p, a_slots, b_slots, kept):
    v, block = a_slots[0, 0, p], kept[0, 0, f]
    wanted = jnp.where((v < 16) & ((v & 12) == (block & 12)), (v & 3) * 4 + (block & 3), -1)
    q = jnp.int32(SLOTS)
    for slot in range(SLOTS):
        q = jnp.where(b_slots[0, 0, slot] == wanted, slot, q)
    return q


def exchange_kernel(a_ref, b_ref, ai_ref, bi_ref, ci_ref, a2_ref, b2_ref, c0_ref, plan_ref, msg, got, slots, a_here, b_here,
                    c_here, l_sems, c_sems, relay, first, second,
                    a_sems, i_sems, up_send, up_recv, on_send, on_recv, b_sems, f_sems, s_sems, h_sems, m_sems, t_sems, g_sems,
                    ready):
    row, col = lax.axis_index("row"), lax.axis_index("col")
    y, z_lo = lax.rem(row, LINES), lax.div(row, LINES)
    core, chip = lax.rem(col, 2), lax.div(col, 2)
    z_hi, x = lax.rem(chip, 4), lax.div(chip, 4)
    z = z_hi * 4 + z_lo
    core0, core1 = core == 0, core == 1

    def place(px, py, pz, pcore):
        pz = lax.rem(pz, ZS)
        return (lax.rem(pz, 4) * LINES + py, (lax.rem(px, 4) * 4 + lax.div(pz, 4)) * 2 + pcore)

    def when(*conditions):
        whole = conditions[0]
        for condition in conditions[1:]:
            whole = whole & condition
        return pl.when(whole)

    def one(*conditions):
        whole = conditions[0]
        for condition in conditions[1:]:
            whole = whole & condition
        return jnp.where(whole, 1, 0)

    a_to, a_from = (row, lax.rem(col + 31, 32)), (row, lax.rem(col + 1, 32))
    relay_to = place(x, y, z + UP, 0)
    sender_z = lax.rem(z + ZS - UP, ZS)
    sender_hi = lax.div(sender_z, 4)
    sender = place(x, y, z + ZS - UP, 0)
    relay_end = place(x + jnp.where(sender_hi == 0, 3, 0), y, sender_z + 12, 1)
    last_relay = place(x + jnp.where(z_hi == 3, 1, 0), y, z + 4 + UP, 0)
    from_z = lax.rem(z + 4, ZS)

    def share(at):
        found = at * 0
        for place_z, count in enumerate(SHARE):
            if count:
                found = found + jnp.where(at == place_z, count, 0)
        return found

    my_share, relay_share, from_share = share(z), share(sender_z), share(from_z)

    sends_up, relays, gets_up = core0 & (my_share > 0), core0 & (relay_share > 0), core1 & (from_share > 0)
    up_late = z + UP < ZS
    in_late = z >= UP
    on_late = z < 4 + UP
    got_late = z >= 12 - UP
    down_late, end_late = z_hi == 0, z_hi == 3
    holds, frees = core0 & (sender_hi == 0) & TURNS, core1 & (z_hi == 0) & TURNS
    held = place(x, y, z + UP, 0)

    z_down, z_up = lax.rem(z_lo + 3, 4) * LINES, lax.rem(z_lo + 1, 4) * LINES
    here = z_lo * LINES
    top, bottom = y == 0, y == LINES - 1
    b_to = (lax.rem(row + 31, 32), col)
    b_from = (lax.rem(row + 1, 32), col)
    col0, col1 = col - core, col - core + 1

    barrier = pltpu.get_barrier_semaphore()

    def greet(device):
        pl.semaphore_signal(barrier, inc=1, device_id=device, device_id_type=MESH)

    @when(~bottom)
    def _():
        greet(b_from)

    @when(core0)
    def _():
        greet(a_from)

    @when(core1, ~end_late)
    def _():
        greet(a_from)

    @when(core0, down_late)
    def _():
        greet(a_to)

    @when(frees)
    def _():
        greet(held)

    @when(sends_up, up_late)
    def _():
        greet(relay_to)

    @when(relays, ~in_late)
    def _():
        greet(sender)

    @when(relays, on_late)
    def _():
        greet(relay_end)

    @when(gets_up, ~got_late)
    def _():
        greet(last_relay)

    @when(top)
    def _():
        for line in range(1, LINES):
            greet((here + line, col1))
        greet((z_down, col1))
        greet(b_to)

    @when(core1, ~top, ~bottom)
    def _():
        greet((z_up + y, col1))

    @when(bottom)
    def _():
        for line in range(LINES - 1):
            greet((here + line, col1))
        greet((z_up + LINES - 1, col1))

    fetch_a = pltpu.make_async_copy(a_ref, a_here, l_sems.at[0])
    fetch_b = pltpu.make_async_copy(b_ref, b_here, l_sems.at[1])
    fetch_a.start()
    fetch_b.start()

    ints = (8, 128)
    lane = lax.broadcasted_iota(jnp.int32, ints, 1)
    for which, source in enumerate((ai_ref, bi_ref)):
        packed = jnp.zeros(ints, jnp.int32)
        for slot in range(SLOTS):
            packed = jnp.where(lane == slot, source[0, 0, slot], packed)
        msg[which] = packed

    greetings = one(~top) + one(core1) + one(core0, ~down_late) + one(core1, end_late)
    greetings = greetings + one(sends_up, ~up_late) + one(relays, in_late) + one(relays, ~on_late)
    greetings = greetings + one(gets_up, got_late) + 4 * one(core1) + one(core1, ~top, ~bottom)
    greetings = greetings + one(bottom) + one(holds)
    @when(greetings > 0)
    def _():
        pl.semaphore_wait(barrier, greetings)

    def tell(which, device):
        pl.semaphore_signal(ready.at[which], inc=1, device_id=device, device_id_type=MESH)

    @when(core1, end_late)
    def _():
        tell(0, a_from)

    @when(holds)
    def _():
        tell(4, place(x, y, z + ZS - UP, 1))

    @when(core1, ~top)
    def _():
        tell(3, (here, col0))
        tell(3, (here, col1))

    @when(core1, top)
    def _():
        tell(3, (z_up, col0))
        tell(3, (z_up, col1))

    @when(bottom)
    def _():
        tell(3, b_from)

    @when(relays, in_late)
    def _():
        tell(1, sender)

    @when(gets_up, got_late)
    def _():
        tell(2, last_relay)

    def remote(src, dst, send, recv, device):
        return pltpu.make_async_remote_copy(src_ref=src, dst_ref=dst, send_sem=send, recv_sem=recv,
                                            device_id=device, device_id_type=MESH)

    def head(g):
        rows = pl.ds(0, ROWS - g * CHUNK)
        return remote(a_ref.at[rows], a2_ref.at[rows], a_sems.at[0], a_sems.at[1], a_to)

    def chunk_rows(g, n):
        return pl.ds(ROWS - g * CHUNK + n * CHUNK, CHUNK)

    def slot_rows(n):
        return pl.ds(n * CHUNK, CHUNK)

    def up(g, n):
        return remote(a_ref.at[chunk_rows(g, n)], relay.at[slot_rows(n)], up_send.at[n], up_recv.at[n], relay_to)

    def on(g, n):
        return remote(relay.at[slot_rows(n)], a2_ref.at[chunk_rows(g, n)], on_send.at[n], on_recv.at[n], relay_end)

    whole = remote(a_ref, a2_ref, a_sems.at[0], a_sems.at[1], a_to)
    ints_a = remote(msg.at[0], got.at[0], i_sems.at[0], i_sems.at[1], a_to)
    ints_b = remote(msg.at[1], got.at[1], i_sems.at[2], i_sems.at[3], b_to)
    b_main = remote(b_ref, b2_ref, b_sems.at[0], b_sems.at[1], b_to)

    def part(line):
        return pl.ds(line * PIECE, PIECE)

    my_part = pl.ds(pl.multiple_of(y * PIECE, PIECE), PIECE)

    def leg_y(line, c):
        return remote(b_ref.at[part(line)], first.at[c], f_sems.at[line], h_sems.at[c], (here + line, col1))

    def leg_z(c):
        return remote(b_ref.at[part(0)], second.at[c], f_sems.at[0], s_sems.at[c], (z_down, col1))

    def then_z(c):
        return remote(first.at[c], second.at[c], m_sems.at[c], s_sems.at[c], (z_down + y, col1))

    def then_end(c):
        return remote(first.at[c], b2_ref.at[part(LINES - 1)], m_sems.at[c], g_sems.at[LINES - 1],
                      (z_down + LINES - 1, col0 + c))

    def then_y(c):
        return remote(second.at[c], b2_ref.at[my_part], t_sems.at[c], g_sems.at[y], (here + LINES - 1, col0 + c))

    def arrival(line):
        return remote(second.at[0], b2_ref.at[part(line)], t_sems.at[0], g_sems.at[line], (here, col))

    def down():
        for g in COUNTS:
            @when(core0, ~down_late, my_share == g)
            def _():
                ints_a.start()
                if g * CHUNK < ROWS:
                    head(g).start()

    if FIRST:
        down()

    @when(core1)
    def _():
        whole.start()

    @when(~top)
    def _():
        b_main.start()
        ints_b.start()

    @when(core1)
    def _():
        ints_a.start()

    if not FIRST:
        down()

    def kept_block(f, carry):
        total = jnp.zeros((BS, BS), jnp.float32)
        for p in range(SLOTS):
            q = wanted_slot(f, p, ai_ref, bi_ref, ci_ref)
            right = jnp.zeros((BS, BS), jnp.float32)
            for slot in range(SLOTS):
                right = jnp.where(q == slot, b_here[pl.ds(slot * BS, BS), :], right)
            total = total + block_product(a_here[pl.ds(p * BS, BS), :], right)
        c_here[f] = total
        return carry

    stores = [pltpu.make_async_copy(c_here.at[f], c0_ref.at[f], c_sems.at[f]) for f in range(F)]

    def early(first_f, last_f):
        lax.fori_loop(first_f, last_f, kept_block, 0)
        for f in range(first_f, last_f):
            stores[f].start()

    fetch_a.wait()
    fetch_b.wait()
    early(0, HALF)

    for c in range(2):
        @when(top, core == c)
        def _():
            pl.semaphore_wait(ready.at[3], LINES + 1)
            for line in (4, 3, 5, 2, 6, 1, 7):
                leg_y(line, c).start()
            leg_z(c).start()
            ints_b.start()

    @when(sends_up, up_late)
    def _():
        pl.semaphore_wait(ready.at[1], 1)

    for g in COUNTS:
        if g:
            @when(core0, my_share == g)
            def _():
                for n in range(g):
                    up(g, n).start()

    @when(core0, down_late)
    def _():
        pl.semaphore_wait(ready.at[0], 1)
        ints_a.start()

    for g in COUNTS:
        if g * CHUNK < ROWS:
            @when(core0, down_late, my_share == g)
            def _():
                head(g).start()

    @when(core0)
    def _():
        early(HALF, F)

    @when(relays, on_late)
    def _():
        pl.semaphore_wait(ready.at[2], 1)

    @when(holds)
    def _():
        pl.semaphore_wait(ready.at[5], 1)

    for g in COUNTS:
        if g:
            @when(core0, relay_share == g)
            def _():
                for n in range(g):
                    up(g, n).wait_recv()
                    on(g, n).start()

    for c in range(2):
        @when(core1, ~top)
        def _():
            leg_y(1, c).wait_recv()

        @when(core1, ~top, ~bottom)
        def _():
            then_z(c).start()

        @when(core1, bottom)
        def _():
            then_end(c).start()

    @when(core1)
    def _():
        early(HALF, F)

    for c in range(2):
        @when(core1, ~bottom)
        def _():
            leg_z(c).wait_recv()
            then_y(c).start()

    for g in COUNTS:
        if g:
            @when(frees, from_share == g)
            def _():
                for n in range(g):
                    on(g, n).wait_recv()

    @when(frees)
    def _():
        pl.semaphore_wait(ready.at[4], 1)
        tell(5, held)

    ints_a.wait()
    ints_b.wait()
    fetch_slots = pltpu.make_async_copy(got, slots, l_sems.at[2])
    fetch_slots.start()
    fetch_slots.wait()
    plan_later(slots, ci_ref, plan_ref)
    for f in range(F):
        met = jnp.int32(0)
        for p in range(SLOTS):
            met = met | jnp.where(wanted_slot(f, p, ai_ref, bi_ref, ci_ref) < SLOTS, 1, 0)
        plan_ref[BEGUN + f] = met

    @when(core1)
    def _():
        whole.wait_send()

    @when(core0)
    def _():
        whole.wait_recv()

    @when(~top)
    def _():
        b_main.wait_send()

    @when(~bottom)
    def _():
        b_main.wait_recv()

    @when(top)
    def _():
        leg_z(0).wait_send()
        for line in range(1, LINES):
            leg_y(line, 0).wait_send()

    for c in range(2):
        @when(core1, ~top)
        def _():
            then_z(c).wait_send()

        @when(core1, ~bottom)
        def _():
            then_y(c).wait_send()

    @when(bottom)
    def _():
        for line in range(LINES):
            arrival(line).wait_recv()

    for g in COUNTS:
        @when(core0, my_share == g)
        def _():
            for n in range(g):
                up(g, n).wait_send()
            if g * CHUNK < ROWS:
                head(g).wait_send()

        @when(core0, relay_share == g)
        def _():
            for n in range(g):
                on(g, n).wait_send()

        @when(core1, from_share == g)
        def _():
            if g * CHUNK < ROWS:
                head(g).wait_recv()

        if g:
            @when(core1, from_share == g, ~frees)
            def _():
                for n in range(g):
                    on(g, n).wait_recv()

    for f in range(F):
        stores[f].wait()


def exchange(a, b, a_index, b_index, c_index):
    panel = jax.ShapeDtypeStruct((ROWS, BS), jnp.float32)
    blocks = jax.ShapeDtypeStruct((F, BS, BS), jnp.float32)
    plan = jax.ShapeDtypeStruct((PLAN,), jnp.int32)
    dma = pltpu.SemaphoreType.DMA
    return pl.pallas_call(
        exchange_kernel,
        out_shape=(panel, panel, blocks, plan),
        in_specs=[HBM, HBM, SMEM, SMEM, SMEM],
        out_specs=(HBM, HBM, HBM, SMEM),
        scratch_shapes=[
            pltpu.VMEM((2, 8, 128), jnp.int32),
            pltpu.VMEM((2, 8, 128), jnp.int32),
            pltpu.SMEM((2, 8, 128), jnp.int32),
            pltpu.VMEM((ROWS, BS), jnp.float32),
            pltpu.VMEM((ROWS, BS), jnp.float32),
            pltpu.VMEM((F, BS, BS), jnp.float32),
            dma((3,)),
            dma((F,)),
            pltpu.VMEM((MOST * CHUNK, BS), jnp.float32),
            pltpu.VMEM((2, PIECE, BS), jnp.float32),
            pltpu.VMEM((2, PIECE, BS), jnp.float32),
            dma((2,)),
            dma((4,)),
            dma((MOST,)),
            dma((MOST,)),
            dma((MOST,)),
            dma((MOST,)),
            dma((2,)),
            dma((LINES,)),
            dma((2,)),
            dma((2,)),
            dma((2,)),
            dma((2,)),
            dma((LINES,)),
            pltpu.SemaphoreType.REGULAR((6,)),
        ],
        compiler_params=pltpu.CompilerParams(collective_id=0, has_side_effects=True, vmem_limit_bytes=VMEM),
        cost_estimate=pl.CostEstimate(flops=6 * F * SLOTS * BS ** 3, bytes_accessed=12 * ROWS * BS * 4, transcendentals=0),
        name="exchange",
    )(a, b, a_index, b_index, c_index)


def product_kernel(c0, a1, b1, plan, out, va, vb, acc, blank, todo, a_sem, b_sem, in_sem, out_sem):
    touched = [plan[TOUCHED + f] for f in range(F)]
    need_a = [plan[NEED_A + p] for p in range(SLOTS)]
    need_b = [plan[NEED_B + q] for q in range(SLOTS)]

    def part(slot):
        return pl.ds(slot * BS, BS)

    fetches = []
    for p in range(SLOTS):
        fetches.append((need_a[p], pltpu.make_async_copy(a1.at[part(p)], va.at[p], a_sem.at[p])))
        fetches.append((need_b[p], pltpu.make_async_copy(b1.at[part(p)], vb.at[p], b_sem.at[p])))
    begun = [plan[BEGUN + f] for f in range(F)]
    for f in range(F):
        fetches.append((begun[f], pltpu.make_async_copy(c0.at[f], acc.at[f], in_sem.at[f])))
    blanks = [pltpu.make_async_copy(blank, out.at[f], out_sem.at[f]) for f in range(F)]
    writes = [pltpu.make_async_copy(acc.at[f], out.at[f], out_sem.at[f]) for f in range(F)]
    for need, copy in fetches:
        pl.when(need != 0)(copy.start)
    blank[...] = jnp.zeros((BS, BS), jnp.float32)
    for f in range(F):
        pl.when((begun[f] | touched[f]) == 0)(blanks[f].start)
    for f in range(F):
        @pl.when((begun[f] == 0) & (touched[f] != 0))
        def _():
            acc[f] = jnp.zeros((BS, BS), jnp.float32)

    count = jnp.int32(0)
    for p in range(SLOTS):
        for q in range(SLOTS):
            place = plan[p * SLOTS + q]
            todo[count] = (p * 4 + q) * 8 + place
            count = count + jnp.where(place < F, 1, 0)

    for need, copy in fetches:
        pl.when(need != 0)(copy.wait)

    def pair(t, carry):
        entry = todo[t]
        f = entry & 7
        acc[f] += block_product(va[entry >> 5], vb[(entry >> 3) & 3])
        return carry

    lax.fori_loop(0, count, pair, 0)
    for f in range(F):
        pl.when((begun[f] | touched[f]) != 0)(writes[f].start)
    for f in range(F):
        writes[f].wait()


def products(c0, a1, b1, plan):
    dma = pltpu.SemaphoreType.DMA
    return pl.pallas_call(
        product_kernel,
        out_shape=jax.ShapeDtypeStruct((F, BS, BS), jnp.float32),
        in_specs=[HBM, HBM, HBM, SMEM],
        out_specs=HBM,
        scratch_shapes=[
            pltpu.VMEM((SLOTS, BS, BS), jnp.float32),
            pltpu.VMEM((SLOTS, BS, BS), jnp.float32),
            pltpu.VMEM((F, BS, BS), jnp.float32),
            pltpu.VMEM((BS, BS), jnp.float32),
            pltpu.SMEM((SLOTS * SLOTS + 1,), jnp.int32),
            dma((SLOTS,)),
            dma((SLOTS,)),
            dma((F,)),
            dma((F,)),
        ],
        compiler_params=pltpu.CompilerParams(vmem_limit_bytes=VMEM),
        cost_estimate=pl.CostEstimate(flops=6 * BS ** 3, bytes_accessed=12 * BS * BS * 4, transcendentals=0),
        name="products",
    )(c0, a1, b1, plan)


def per_device(a_panels, a_index, b_panels, b_index, c_index):
    a0 = a_panels.reshape(ROWS, BS)
    b0 = b_panels.reshape(ROWS, BS)
    a1, b1, c0, plan = exchange(a0, b0, a_index, b_index, c_index)
    blocks = products(c0, a1, b1, plan)
    return blocks[None, None]


def solution(mesh):
    return jax.shard_map(
        per_device,
        mesh=mesh,
        in_specs=(
            P("row", "col", None, None, None),
            P("row", "col", None),
            P("row", "col", None, None, None),
            P("row", "col", None),
            P("row", "col", None),
        ),
        out_specs=P("row", "col", None, None, None),
        check_vma=False,
    )
```

time: 53.1 us -> 50.8 us (0.957)
  the two profiles are of different devices: /device:TPU:119 before, /device:TPU:127 now
where the time goes in v3:
time: 50.8 us; the launch traced here: 50.6 us
  Pallas kernels  50.5 us (99%)
    pallas_call x1, Pallas kernels, exchange(): pl.pallas_call(exchange_kernel, out_shape=(panel, panel, blocks, plan), i...  46.9 us
    pallas_call x1, Pallas kernels, products(): pl.pallas_call(product_kernel, out_shape=jax.ShapeDtypeStruct((F, BS, BS)...  3.67 us

profile of v3, /device:TPU:127, one launch (start us, length us, event | category | flops | bytes accessed | tf_op | source)
XLA Modules:
  0.0 50.6 jit_solution(14786638203612795510)
XLA Ops:
  0.0 46.9 %exchange.1 = (f32[768,256]{1,0:T(8,128)}, f32[768,256]{1,0:T(8,128)}, f32[6,256,256]{2,1,0:T(8,128)}, s32[27]{0:T(128)}) custom-call(f32[768,256]{1,0:T(8,128)} %bitcast.3, f32[768,256]{1,0:T(8,128)} %bitcast.4, s32[1,1,3]{2,1,0:T(1,128)} %ai_ref.1, s32[1,1,3]{2,1,0:T(1,128)} %bi_ref.1, s32[1,1,6]{2,1,0:T(1,128)} %ci_ref.1), custom_call_target="tpu_custom_call" | custom-call | flops 1811939328 | bytes 9437184 | tf_op jit(solution)/shard_map/exchange/pallas_call | solution.py:519
  46.9 3.7 %products.1 = f32[6,256,256]{2,1,0:T(8,128)} custom-call(f32[6,256,256]{2,1,0:T(8,128)} %get-tuple-element.9.c0, f32[768,256]{1,0:T(8,128)} %get-tuple-element.10.a1, f32[768,256]{1,0:T(8,128)} %get-tuple-element.11.b1, s32[27]{0:T(128)} %get-tuple-element.12.plan), custom_call_target="tpu_custom_call" | custom-call | flops 100663296 | bytes 3145728 | tf_op jit(solution)/shard_map/products/pallas_call | solution.py:609

commit v4 on v3

--- a/solution.py
+++ b/solution.py
@@ -12,18 +12,14 @@
 LINES = 8
 ZS = 16
 CHUNK = 96
-SHARE = (4, 4, 4, 4, 0, 0, 0, 2, 2, 2, 0, 2, 0, 0, 0, 0)
+SHARE = (4, 4, 4, 4, 0, 0, 1, 2, 2, 2, 0, 2, 0, 0, 0, 0)
 COUNTS = sorted(set(SHARE))
-TURNS = False
-FIRST = False
 MOST = max(1, max(SHARE))
-UP = 5
+UP = 6
 PIECE = ROWS // LINES
 VMEM = 60 * 1024 * 1024
 
-NEED_A = SLOTS * SLOTS
-NEED_B = NEED_A + SLOTS
-TOUCHED = NEED_B + SLOTS
+TOUCHED = SLOTS * SLOTS
 BEGUN = TOUCHED + F
 PLAN = BEGUN + F
 HALF = F // 2
@@ -45,11 +41,9 @@
 
 
 def plan_later(slots, kept, plan):
-    need_b = [jnp.int32(0)] * SLOTS
     touched = [jnp.int32(0)] * F
     for p in range(SLOTS):
         v = slots[0, 0, p]
-        need_a = jnp.int32(0)
         for q in range(SLOTS):
             w = slots[1, 0, q]
             target = jnp.where((v < 16) & (w < 16) & ((v & 3) == (w >> 2)), (v & 12) + (w & 3), -1)
@@ -58,13 +52,7 @@
                 mine = kept[0, 0, f] == target
                 place = jnp.where(mine, f, place)
                 touched[f] = jnp.where(mine, 1, touched[f])
-            hit = jnp.where(place < F, 1, 0)
             plan[p * SLOTS + q] = place
-            need_a = need_a | hit
-            need_b[q] = need_b[q] | hit
-        plan[NEED_A + p] = need_a
-    for q in range(SLOTS):
-        plan[NEED_B + q] = need_b[q]
     for f in range(F):
         plan[TOUCHED + f] = touched[f]
 
@@ -129,8 +117,6 @@
     on_late = z < 4 + UP
     got_late = z >= 12 - UP
     down_late, end_late = z_hi == 0, z_hi == 3
-    holds, frees = core0 & (sender_hi == 0) & TURNS, core1 & (z_hi == 0) & TURNS
-    held = place(x, y, z + UP, 0)
 
     z_down, z_up = lax.rem(z_lo + 3, 4) * LINES, lax.rem(z_lo + 1, 4) * LINES
     here = z_lo * LINES
@@ -159,10 +145,6 @@
     @when(core0, down_late)
     def _():
         greet(a_to)
-
-    @when(frees)
-    def _():
-        greet(held)
 
     @when(sends_up, up_late)
     def _():
@@ -213,7 +195,7 @@
     greetings = one(~top) + one(core1) + one(core0, ~down_late) + one(core1, end_late)
     greetings = greetings + one(sends_up, ~up_late) + one(relays, in_late) + one(relays, ~on_late)
     greetings = greetings + one(gets_up, got_late) + 4 * one(core1) + one(core1, ~top, ~bottom)
-    greetings = greetings + one(bottom) + one(holds)
+    greetings = greetings + one(bottom)
     @when(greetings > 0)
     def _():
         pl.semaphore_wait(barrier, greetings)
@@ -224,10 +206,6 @@
     @when(core1, end_late)
     def _():
         tell(0, a_from)
-
-    @when(holds)
-    def _():
-        tell(4, place(x, y, z + ZS - UP, 1))
 
     @when(core1, ~top)
     def _():
@@ -300,17 +278,6 @@
     def arrival(line):
         return remote(second.at[0], b2_ref.at[part(line)], t_sems.at[0], g_sems.at[line], (here, col))
 
-    def down():
-        for g in COUNTS:
-            @when(core0, ~down_late, my_share == g)
-            def _():
-                ints_a.start()
-                if g * CHUNK < ROWS:
-                    head(g).start()
-
-    if FIRST:
-        down()
-
     @when(core1)
     def _():
         whole.start()
@@ -324,8 +291,12 @@
     def _():
         ints_a.start()
 
-    if not FIRST:
-        down()
+    for g in COUNTS:
+        @when(core0, ~down_late, my_share == g)
+        def _():
+            ints_a.start()
+            if g * CHUNK < ROWS:
+                head(g).start()
 
     def kept_block(f, carry):
         total = jnp.zeros((BS, BS), jnp.float32)
@@ -388,10 +359,6 @@
     def _():
         pl.semaphore_wait(ready.at[2], 1)
 
-    @when(holds)
-    def _():
-        pl.semaphore_wait(ready.at[5], 1)
-
     for g in COUNTS:
         if g:
             @when(core0, relay_share == g)
@@ -423,18 +390,6 @@
             leg_z(c).wait_recv()
             then_y(c).start()
 
-    for g in COUNTS:
-        if g:
-            @when(frees, from_share == g)
-            def _():
-                for n in range(g):
-                    on(g, n).wait_recv()
-
-    @when(frees)
-    def _():
-        pl.semaphore_wait(ready.at[4], 1)
-        tell(5, held)
-
     ints_a.wait()
     ints_b.wait()
     fetch_slots = pltpu.make_async_copy(got, slots, l_sems.at[2])
@@ -502,7 +457,7 @@
                 head(g).wait_recv()
 
         if g:
-            @when(core1, from_share == g, ~frees)
+            @when(core1, from_share == g)
             def _():
                 for n in range(g):
                     on(g, n).wait_recv()
@@ -546,7 +501,7 @@
             dma((2,)),
             dma((2,)),
             dma((LINES,)),
-            pltpu.SemaphoreType.REGULAR((6,)),
+            pltpu.SemaphoreType.REGULAR((4,)),
         ],
         compiler_params=pltpu.CompilerParams(collective_id=0, has_side_effects=True, vmem_limit_bytes=VMEM),
         cost_estimate=pl.CostEstimate(flops=6 * F * SLOTS * BS ** 3, bytes_accessed=12 * ROWS * BS * 4, transcendentals=0),
@@ -554,26 +509,21 @@
     )(a, b, a_index, b_index, c_index)
 
 
-def product_kernel(c0, a1, b1, plan, out, va, vb, acc, blank, todo, a_sem, b_sem, in_sem, out_sem):
+def product_kernel(c0, a1, b1, plan_ref, out, plan, va, vb, acc, blank, todo, p_sem, a_sem, b_sem, in_sem, out_sem):
+    fetch_plan = pltpu.make_async_copy(plan_ref, plan, p_sem)
+    fetch_plan.start()
+    fetches = [pltpu.make_async_copy(a1, va, a_sem), pltpu.make_async_copy(b1, vb, b_sem)]
+    for copy in fetches:
+        copy.start()
+    blank[...] = jnp.zeros((BS, BS), jnp.float32)
+    fetch_plan.wait()
     touched = [plan[TOUCHED + f] for f in range(F)]
-    need_a = [plan[NEED_A + p] for p in range(SLOTS)]
-    need_b = [plan[NEED_B + q] for q in range(SLOTS)]
-
-    def part(slot):
-        return pl.ds(slot * BS, BS)
-
-    fetches = []
-    for p in range(SLOTS):
-        fetches.append((need_a[p], pltpu.make_async_copy(a1.at[part(p)], va.at[p], a_sem.at[p])))
-        fetches.append((need_b[p], pltpu.make_async_copy(b1.at[part(p)], vb.at[p], b_sem.at[p])))
     begun = [plan[BEGUN + f] for f in range(F)]
-    for f in range(F):
-        fetches.append((begun[f], pltpu.make_async_copy(c0.at[f], acc.at[f], in_sem.at[f])))
+    starts = [pltpu.make_async_copy(c0.at[f], acc.at[f], in_sem.at[f]) for f in range(F)]
     blanks = [pltpu.make_async_copy(blank, out.at[f], out_sem.at[f]) for f in range(F)]
     writes = [pltpu.make_async_copy(acc.at[f], out.at[f], out_sem.at[f]) for f in range(F)]
-    for need, copy in fetches:
-        pl.when(need != 0)(copy.start)
-    blank[...] = jnp.zeros((BS, BS), jnp.float32)
+    for f in range(F):
+        pl.when(begun[f] != 0)(starts[f].start)
     for f in range(F):
         pl.when((begun[f] | touched[f]) == 0)(blanks[f].start)
     for f in range(F):
@@ -588,18 +538,24 @@
             todo[count] = (p * 4 + q) * 8 + place
             count = count + jnp.where(place < F, 1, 0)
 
-    for need, copy in fetches:
-        pl.when(need != 0)(copy.wait)
+    for f in range(F):
+        pl.when(begun[f] != 0)(starts[f].wait)
+    for f in range(F):
+        pl.when((begun[f] != 0) & (touched[f] == 0))(writes[f].start)
+    for copy in fetches:
+        copy.wait()
 
     def pair(t, carry):
         entry = todo[t]
         f = entry & 7
-        acc[f] += block_product(va[entry >> 5], vb[(entry >> 3) & 3])
+        left = va[pl.ds(pl.multiple_of((entry >> 5) * BS, BS), BS), :]
+        right = vb[pl.ds(pl.multiple_of(((entry >> 3) & 3) * BS, BS), BS), :]
+        acc[f] += block_product(left, right)
         return carry
 
     lax.fori_loop(0, count, pair, 0)
     for f in range(F):
-        pl.when((begun[f] | touched[f]) != 0)(writes[f].start)
+        pl.when(touched[f] != 0)(writes[f].start)
     for f in range(F):
         writes[f].wait()
 
@@ -609,16 +565,18 @@
     return pl.pallas_call(
         product_kernel,
         out_shape=jax.ShapeDtypeStruct((F, BS, BS), jnp.float32),
-        in_specs=[HBM, HBM, HBM, SMEM],
+        in_specs=[HBM, HBM, HBM, HBM],
         out_specs=HBM,
         scratch_shapes=[
-            pltpu.VMEM((SLOTS, BS, BS), jnp.float32),
-            pltpu.VMEM((SLOTS, BS, BS), jnp.float32),
+            pltpu.SMEM((PLAN,), jnp.int32),
+            pltpu.VMEM((ROWS, BS), jnp.float32),
+            pltpu.VMEM((ROWS, BS), jnp.float32),
             pltpu.VMEM((F, BS, BS), jnp.float32),
             pltpu.VMEM((BS, BS), jnp.float32),
             pltpu.SMEM((SLOTS * SLOTS + 1,), jnp.int32),
-            dma((SLOTS,)),
-            dma((SLOTS,)),
+            dma,
+            dma,
+            dma,
             dma((F,)),
             dma((F,)),
         ],

time: 50.8 us -> 49 us (0.965)
  Pallas kernels: 50.5 us -> 48.3 us
    pallas_call x1, Pallas kernels: 3.67 us -> 2.5 us  [products(): pl.pallas_call(product_kernel, out_shape=jax.ShapeDtypeStruct((F, BS, BS)...]
    pallas_call x1, Pallas kernels: 46.9 us -> 45.8 us  [exchange(): pl.pallas_call(exchange_kernel, out_shape=(panel, panel, blocks, plan), i...]
where the time goes in v4:
time: 49 us; the launch traced here: 48.3 us
  Pallas kernels  48.3 us (99%)
    pallas_call x1, Pallas kernels, exchange(): pl.pallas_call(exchange_kernel, out_shape=(panel, panel, blocks, plan), i...  45.8 us
    pallas_call x1, Pallas kernels, products(): pl.pallas_call(product_kernel, out_shape=jax.ShapeDtypeStruct((F, BS, BS)...  2.5 us

profile of v4, /device:TPU:127, one launch (start us, length us, event | category | flops | bytes accessed | tf_op | source)
XLA Modules:
  0.0 48.3 jit_solution(15975655263053523620)
XLA Ops:
  0.0 45.8 %exchange.1 = (f32[768,256]{1,0:T(8,128)}, f32[768,256]{1,0:T(8,128)}, f32[6,256,256]{2,1,0:T(8,128)}, s32[21]{0:T(128)}) custom-call(f32[768,256]{1,0:T(8,128)} %bitcast.3, f32[768,256]{1,0:T(8,128)} %bitcast.4, s32[1,1,3]{2,1,0:T(1,128)} %ai_ref.1, s32[1,1,3]{2,1,0:T(1,128)} %bi_ref.1, s32[1,1,6]{2,1,0:T(1,128)} %ci_ref.1), custom_call_target="tpu_custom_call" | custom-call | flops 1811939328 | bytes 9437184 | tf_op jit(solution)/shard_map/exchange/pallas_call | solution.py:474
  45.8 2.5 %products.1 = f32[6,256,256]{2,1,0:T(8,128)} custom-call(f32[6,256,256]{2,1,0:T(8,128)} %get-tuple-element.9.c0, f32[768,256]{1,0:T(8,128)} %get-tuple-element.10.a1, f32[768,256]{1,0:T(8,128)} %get-tuple-element.11.b1, s32[21]{0:T(128)} %get-tuple-element.12.plan_ref), custom_call_target="tpu_custom_call" | custom-call | flops 100663296 | bytes 3145728 | tf_op jit(solution)/shard_map/products/pallas_call | solution.py:565

commit v5 on v4

--- a/solution.py
+++ b/solution.py
@@ -20,8 +20,7 @@
 VMEM = 60 * 1024 * 1024
 
 TOUCHED = SLOTS * SLOTS
-BEGUN = TOUCHED + F
-PLAN = BEGUN + F
+PLAN = TOUCHED + F
 HALF = F // 2
 
 MESH = pl.DeviceIdType.MESH
@@ -396,11 +395,6 @@
     fetch_slots.start()
     fetch_slots.wait()
     plan_later(slots, ci_ref, plan_ref)
-    for f in range(F):
-        met = jnp.int32(0)
-        for p in range(SLOTS):
-            met = met | jnp.where(wanted_slot(f, p, ai_ref, bi_ref, ci_ref) < SLOTS, 1, 0)
-        plan_ref[BEGUN + f] = met
 
     @when(core1)
     def _():
@@ -509,28 +503,16 @@
     )(a, b, a_index, b_index, c_index)
 
 
-def product_kernel(c0, a1, b1, plan_ref, out, plan, va, vb, acc, blank, todo, p_sem, a_sem, b_sem, in_sem, out_sem):
+def product_kernel(c0, a1, b1, plan_ref, out, plan, va, vb, acc, todo, p_sem, a_sem, b_sem, in_sem, out_sem):
     fetch_plan = pltpu.make_async_copy(plan_ref, plan, p_sem)
     fetch_plan.start()
+    starts = [pltpu.make_async_copy(c0.at[f], acc.at[f], in_sem.at[f]) for f in range(F)]
+    writes = [pltpu.make_async_copy(acc.at[f], out.at[f], out_sem.at[f]) for f in range(F)]
     fetches = [pltpu.make_async_copy(a1, va, a_sem), pltpu.make_async_copy(b1, vb, b_sem)]
-    for copy in fetches:
+    for copy in starts + fetches:
         copy.start()
-    blank[...] = jnp.zeros((BS, BS), jnp.float32)
     fetch_plan.wait()
     touched = [plan[TOUCHED + f] for f in range(F)]
-    begun = [plan[BEGUN + f] for f in range(F)]
-    starts = [pltpu.make_async_copy(c0.at[f], acc.at[f], in_sem.at[f]) for f in range(F)]
-    blanks = [pltpu.make_async_copy(blank, out.at[f], out_sem.at[f]) for f in range(F)]
-    writes = [pltpu.make_async_copy(acc.at[f], out.at[f], out_sem.at[f]) for f in range(F)]
-    for f in range(F):
-        pl.when(begun[f] != 0)(starts[f].start)
-    for f in range(F):
-        pl.when((begun[f] | touched[f]) == 0)(blanks[f].start)
-    for f in range(F):
-        @pl.when((begun[f] == 0) & (touched[f] != 0))
-        def _():
-            acc[f] = jnp.zeros((BS, BS), jnp.float32)
-
     count = jnp.int32(0)
     for p in range(SLOTS):
         for q in range(SLOTS):
@@ -539,9 +521,8 @@
             count = count + jnp.where(place < F, 1, 0)
 
     for f in range(F):
-        pl.when(begun[f] != 0)(starts[f].wait)
-    for f in range(F):
-        pl.when((begun[f] != 0) & (touched[f] == 0))(writes[f].start)
+        starts[f].wait()
+        pl.when(touched[f] == 0)(writes[f].start)
     for copy in fetches:
         copy.wait()
 
@@ -572,7 +553,6 @@
             pltpu.VMEM((ROWS, BS), jnp.float32),
             pltpu.VMEM((ROWS, BS), jnp.float32),
             pltpu.VMEM((F, BS, BS), jnp.float32),
-            pltpu.VMEM((BS, BS), jnp.float32),
             pltpu.SMEM((SLOTS * SLOTS + 1,), jnp.int32),
             dma,
             dma,

time: 49 us -> 48.9 us (level)
  the two profiles are of different devices: /device:TPU:127 before, /device:TPU:123 now
where the time goes in v5:
time: 48.9 us; the launch traced here: 48 us
  Pallas kernels  48 us (98%)
    pallas_call x1, Pallas kernels, exchange(): pl.pallas_call(exchange_kernel, out_shape=(panel, panel, blocks, plan), i...  45.8 us
    pallas_call x1, Pallas kernels, products(): pl.pallas_call(product_kernel, out_shape=jax.ShapeDtypeStruct((F, BS, BS)...  2.22 us

profile of v5, /device:TPU:123, one launch (start us, length us, event | category | flops | bytes accessed | tf_op | source)
XLA Modules:
  0.0 48.0 jit_solution(12492109170827451755)
XLA Ops:
  0.0 45.8 %exchange.1 = (f32[768,256]{1,0:T(8,128)}, f32[768,256]{1,0:T(8,128)}, f32[6,256,256]{2,1,0:T(8,128)}, s32[15]{0:T(128)}) custom-call(f32[768,256]{1,0:T(8,128)} %bitcast.3, f32[768,256]{1,0:T(8,128)} %bitcast.4, s32[1,1,3]{2,1,0:T(1,128)} %ai_ref.1, s32[1,1,3]{2,1,0:T(1,128)} %bi_ref.1, s32[1,1,6]{2,1,0:T(1,128)} %ci_ref.1), custom_call_target="tpu_custom_call" | custom-call | flops 1811939328 | bytes 9437184 | tf_op jit(solution)/shard_map/exchange/pallas_call | solution.py:468
  45.8 2.2 %products.1 = f32[6,256,256]{2,1,0:T(8,128)} custom-call(f32[6,256,256]{2,1,0:T(8,128)} %get-tuple-element.9.c0, f32[768,256]{1,0:T(8,128)} %get-tuple-element.10.a1, f32[768,256]{1,0:T(8,128)} %get-tuple-element.11.b1, s32[15]{0:T(128)} %get-tuple-element.12.plan_ref), custom_call_target="tpu_custom_call" | custom-call | flops 100663296 | bytes 3145728 | tf_op jit(solution)/shard_map/products/pallas_call | solution.py:546

commit v6 on v5

--- a/solution.py
+++ b/solution.py
@@ -13,7 +13,10 @@
 ZS = 16
 CHUNK = 96
 SHARE = (4, 4, 4, 4, 0, 0, 1, 2, 2, 2, 0, 2, 0, 0, 0, 0)
+SIDE = (0, 0, 0, 0, 6, 2, 0, 0, 0, 0, 0, 0, 0, 0, 0, 0)
 COUNTS = sorted(set(SHARE))
+PAIRS = sorted(set(zip(SHARE, SIDE)))
+ALL = ROWS // CHUNK
 MOST = max(1, max(SHARE))
 UP = 6
 PIECE = ROWS // LINES
@@ -21,7 +24,7 @@
 
 TOUCHED = SLOTS * SLOTS
 PLAN = TOUCHED + F
-HALF = F // 2
+HALF = 0
 
 MESH = pl.DeviceIdType.MESH
 HBM = pl.BlockSpec(memory_space=pltpu.HBM)
@@ -66,7 +69,7 @@
 
 
 def exchange_kernel(a_ref, b_ref, ai_ref, bi_ref, ci_ref, a2_ref, b2_ref, c0_ref, plan_ref, msg, got, slots, a_here, b_here,
-                    c_here, l_sems, c_sems, relay, first, second,
+                    c_here, beside, l_sems, c_sems, relay, first, second,
                     a_sems, i_sems, up_send, up_recv, on_send, on_recv, b_sems, f_sems, s_sems, h_sems, m_sems, t_sems, g_sems,
                     ready):
     row, col = lax.axis_index("row"), lax.axis_index("col")
@@ -101,14 +104,16 @@
     last_relay = place(x + jnp.where(z_hi == 3, 1, 0), y, z + 4 + UP, 0)
     from_z = lax.rem(z + 4, ZS)
 
-    def share(at):
+    def share(at, table=SHARE):
         found = at * 0
-        for place_z, count in enumerate(SHARE):
+        for place_z, count in enumerate(table):
             if count:
                 found = found + jnp.where(at == place_z, count, 0)
         return found
 
     my_share, relay_share, from_share = share(z), share(sender_z), share(from_z)
+    my_side, from_side = share(z, SIDE), share(from_z, SIDE)
+    side_to, side_from = (row, lax.rem(col + 30, 32)), (row, lax.rem(col + 2, 32))
 
     sends_up, relays, gets_up = core0 & (my_share > 0), core0 & (relay_share > 0), core1 & (from_share > 0)
     up_late = z + UP < ZS
@@ -140,6 +145,14 @@
     @when(core1, ~end_late)
     def _():
         greet(a_from)
+
+    @when(core1, from_side > 0)
+    def _():
+        greet(side_from)
+
+    @when(core1, my_side > 0)
+    def _():
+        greet((row, col0))
 
     @when(core0, down_late)
     def _():
@@ -194,7 +207,7 @@
     greetings = one(~top) + one(core1) + one(core0, ~down_late) + one(core1, end_late)
     greetings = greetings + one(sends_up, ~up_late) + one(relays, in_late) + one(relays, ~on_late)
     greetings = greetings + one(gets_up, got_late) + 4 * one(core1) + one(core1, ~top, ~bottom)
-    greetings = greetings + one(bottom)
+    greetings = greetings + one(bottom) + one(my_side > 0)
     @when(greetings > 0)
     def _():
         pl.semaphore_wait(barrier, greetings)
@@ -232,9 +245,17 @@
         return pltpu.make_async_remote_copy(src_ref=src, dst_ref=dst, send_sem=send, recv_sem=recv,
                                             device_id=device, device_id_type=MESH)
 
-    def head(g):
-        rows = pl.ds(0, ROWS - g * CHUNK)
+    def head(g, side):
+        rows = pl.ds(0, (ALL - g - side) * CHUNK)
         return remote(a_ref.at[rows], a2_ref.at[rows], a_sems.at[0], a_sems.at[1], a_to)
+
+    def across(g, side):
+        rows = pl.ds((ALL - g - side) * CHUNK, side * CHUNK)
+        return remote(a_ref.at[rows], beside.at[pl.ds(0, side * CHUNK)], a_sems.at[2], a_sems.at[3], (row, col1))
+
+    def aside(g, side):
+        rows = pl.ds((ALL - g - side) * CHUNK, side * CHUNK)
+        return remote(beside.at[pl.ds(0, side * CHUNK)], a2_ref.at[rows], a_sems.at[4], a_sems.at[5], side_to)
 
     def chunk_rows(g, n):
         return pl.ds(ROWS - g * CHUNK + n * CHUNK, CHUNK)
@@ -290,12 +311,24 @@
     def _():
         ints_a.start()
 
-    for g in COUNTS:
-        @when(core0, ~down_late, my_share == g)
-        def _():
-            ints_a.start()
-            if g * CHUNK < ROWS:
-                head(g).start()
+    for g, side in PAIRS:
+        @when(core0, my_share == g, my_side == side)
+        def _():
+            if side:
+                across(g, side).start()
+
+            @when(~down_late)
+            def _():
+                ints_a.start()
+                if g + side < ALL:
+                    head(g, side).start()
+
+    for g, side in PAIRS:
+        if side:
+            @when(core1, my_share == g, my_side == side)
+            def _():
+                across(g, side).wait_recv()
+                aside(g, side).start()
 
     def kept_block(f, carry):
         total = jnp.zeros((BS, BS), jnp.float32)
@@ -344,11 +377,11 @@
         pl.semaphore_wait(ready.at[0], 1)
         ints_a.start()
 
-    for g in COUNTS:
-        if g * CHUNK < ROWS:
-            @when(core0, down_late, my_share == g)
-            def _():
-                head(g).start()
+    for g, side in PAIRS:
+        if g + side < ALL:
+            @when(core0, down_late, my_share == g, my_side == side)
+            def _():
+                head(g, side).start()
 
     @when(core0)
     def _():
@@ -432,25 +465,35 @@
         for line in range(LINES):
             arrival(line).wait_recv()
 
-    for g in COUNTS:
-        @when(core0, my_share == g)
+    for g, side in PAIRS:
+        @when(core0, my_share == g, my_side == side)
         def _():
             for n in range(g):
                 up(g, n).wait_send()
-            if g * CHUNK < ROWS:
-                head(g).wait_send()
-
-        @when(core0, relay_share == g)
-        def _():
-            for n in range(g):
-                on(g, n).wait_send()
-
-        @when(core1, from_share == g)
-        def _():
-            if g * CHUNK < ROWS:
-                head(g).wait_recv()
-
+            if g + side < ALL:
+                head(g, side).wait_send()
+            if side:
+                across(g, side).wait_send()
+
+        @when(core1, from_share == g, from_side == side)
+        def _():
+            if g + side < ALL:
+                head(g, side).wait_recv()
+            if side:
+                aside(g, side).wait_recv()
+
+        if side:
+            @when(core1, my_share == g, my_side == side)
+            def _():
+                aside(g, side).wait_send()
+
+    for g in COUNTS:
         if g:
+            @when(core0, relay_share == g)
+            def _():
+                for n in range(g):
+                    on(g, n).wait_send()
+
             @when(core1, from_share == g)
             def _():
                 for n in range(g):
@@ -477,12 +520,13 @@
             pltpu.VMEM((ROWS, BS), jnp.float32),
             pltpu.VMEM((ROWS, BS), jnp.float32),
             pltpu.VMEM((F, BS, BS), jnp.float32),
+            pltpu.VMEM((max(1, max(SIDE)) * CHUNK, BS), jnp.float32),
             dma((3,)),
             dma((F,)),
             pltpu.VMEM((MOST * CHUNK, BS), jnp.float32),
             pltpu.VMEM((2, PIECE, BS), jnp.float32),
             pltpu.VMEM((2, PIECE, BS), jnp.float32),
-            dma((2,)),
+            dma((6,)),
             dma((4,)),
             dma((MOST,)),
             dma((MOST,)),

time: 48.9 us -> 49.2 us (level)
  the two profiles are of different devices: /device:TPU:123 before, /device:TPU:121 now
where the time goes in v6:
time: 49.2 us; the launch traced here: 48.8 us
  Pallas kernels  48.8 us (99%)
    pallas_call x1, Pallas kernels, exchange(): pl.pallas_call(exchange_kernel, out_shape=(panel, panel, blocks, plan), i...  45.9 us
    pallas_call x1, Pallas kernels, products(): pl.pallas_call(product_kernel, out_shape=jax.ShapeDtypeStruct((F, BS, BS)...  2.97 us

profile of v6, /device:TPU:121, one launch (start us, length us, event | category | flops | bytes accessed | tf_op | source)
XLA Modules:
  0.0 48.8 jit_solution(7274259712209944671)
XLA Ops:
  0.0 45.9 %exchange.1 = (f32[768,256]{1,0:T(8,128)}, f32[768,256]{1,0:T(8,128)}, f32[6,256,256]{2,1,0:T(8,128)}, s32[15]{0:T(128)}) custom-call(f32[768,256]{1,0:T(8,128)} %bitcast.3, f32[768,256]{1,0:T(8,128)} %bitcast.4, s32[1,1,3]{2,1,0:T(1,128)} %ai_ref.1, s32[1,1,3]{2,1,0:T(1,128)} %bi_ref.1, s32[1,1,6]{2,1,0:T(1,128)} %ci_ref.1), custom_call_target="tpu_custom_call" | custom-call | flops 1811939328 | bytes 9437184 | tf_op jit(solution)/shard_map/exchange/pallas_call | solution.py:511
  45.9 3.0 %products.1 = f32[6,256,256]{2,1,0:T(8,128)} custom-call(f32[6,256,256]{2,1,0:T(8,128)} %get-tuple-element.9.c0, f32[768,256]{1,0:T(8,128)} %get-tuple-element.10.a1, f32[768,256]{1,0:T(8,128)} %get-tuple-element.11.b1, s32[15]{0:T(128)} %get-tuple-element.12.plan_ref), custom_call_target="tpu_custom_call" | custom-call | flops 100663296 | bytes 3145728 | tf_op jit(solution)/shard_map/products/pallas_call | solution.py:590
